TPU v7x, 128 devices: a whole 4x4x4 slice. The times are simulated.
128 devices in a mesh: grp: 32 (over x, y, z_hi), tp: 4 (over z_lo, core).
Axes of the slice: x: 4, y: 4, z: 4 (z_hi: 2, z_lo: 2; z = z_hi * 2 + z_lo), core: 2. Of those that a mesh axis runs over, the one named last changes fastest.
Arguments:
- queries: bfloat16 [256, 4, 128, 192], P('grp', None, 'tp'), may hold values from -500 to 500
- new_kv: bfloat16 [256, 4, 576], P('grp'), may hold values from -8 to 8
- owner_index: int32 [1], replicated, may hold values from 0 to 31
- prefix_latent: bfloat16 [32, 8192, 512], P('grp'), may hold values from -6 to 6
- prefix_rope: bfloat16 [32, 64, 8192], P('grp'), may hold values from -6 to 6
- key_up: bfloat16 [128, 128, 512], P('tp'), may hold values from -0.25 to 0.25
- value_up: bfloat16 [128, 512, 128], P('tp'), may hold values from -0.25 to 0.25
- out_weight: bfloat16 [16384, 7168], P('tp', 'grp'), may hold values from -2.5 to 2.5
Outputs:
- layer_out: bfloat16 [256, 4, 7168], P('tp', None, 'grp')
All inputs are finite; a program needn't handle non-finite values.
Results may differ from a plain program's by a relative error of at most 0.015.
Values may be sent and summed in bfloat16 or wider, within the bound.
A program may use at most 192 MiB of HBM per device.

v0:
```python
import jax
import jax.numpy as jnp
from jax import lax
from jax.sharding import PartitionSpec as P


def broadcast(x, axis, root):
    mine = lax.axis_index(axis) == root
    return lax.psum(jnp.where(mine, x, jnp.zeros_like(x)), axis)


def body(queries, new_kv, owner_index, prefix_latent, prefix_rope, key_up, value_up, out_weight):
    samp_local, step_count, heads_local, query_width = queries.shape
    nope_width = key_up.shape[1]
    latent_width = key_up.shape[2]
    score_scale = query_width ** (-0.5)
    source_index = owner_index[0]
    latent, rotary = (
        broadcast(prefix_latent[0], "grp", source_index),
        broadcast(prefix_rope[0], "grp", source_index),
    )
    q_nope = queries[:, :, :, :nope_width]
    q_rope = queries[:, :, :, nope_width:]
    q_latent = jnp.einsum(
        "sthn,hnl->sthl", q_nope, key_up, preferred_element_type=jnp.float32
    ).astype(jnp.bfloat16)
    row_count = samp_local * step_count * heads_local
    flat_latent = q_latent.reshape(row_count, latent_width)
    flat_rope = q_rope.reshape(row_count, query_width - nope_width)
    prefix_scores = lax.dot_general(
        flat_latent, latent, (((1,), (1,)), ((), ())), preferred_element_type=jnp.float32
    )
    prefix_scores = (
        prefix_scores + jnp.dot(flat_rope, rotary, preferred_element_type=jnp.float32)
    ) * score_scale
    new_latent = new_kv[:, :, :latent_width]
    new_rope = new_kv[:, :, latent_width:]
    new_scores = jnp.einsum(
        "sthl,sul->sthu", q_latent, new_latent, preferred_element_type=jnp.float32
    )
    new_scores = (
        new_scores
        + jnp.einsum("sthr,sur->sthu", q_rope, new_rope, preferred_element_type=jnp.float32)
    ) * score_scale
    visible = (jnp.arange(step_count)[None, :] <= jnp.arange(step_count)[:, None])[None, :, None, :]
    masked = jnp.where(visible, new_scores, -jnp.inf)
    row_max = jnp.maximum(
        jnp.max(prefix_scores, axis=1), jnp.max(masked, axis=3).reshape(row_count)
    )
    prefix_exp = jnp.exp(prefix_scores - row_max[:, None])
    new_exp = jnp.where(
        visible,
        jnp.exp(masked - row_max.reshape(samp_local, step_count, heads_local)[:, :, :, None]),
        0.0,
    )
    exp_total = jnp.sum(prefix_exp, axis=1) + jnp.sum(new_exp, axis=3).reshape(row_count)
    context = jnp.dot(prefix_exp.astype(jnp.bfloat16), latent, preferred_element_type=jnp.float32)
    new_context = jnp.einsum(
        "sthu,sul->sthl",
        new_exp.astype(jnp.bfloat16),
        new_latent,
        preferred_element_type=jnp.float32,
    )
    context = (context + new_context.reshape(row_count, latent_width)) / exp_total[:, None]
    context = context.astype(jnp.bfloat16).reshape(
        samp_local, step_count, heads_local, latent_width
    )
    attended = jnp.einsum(
        "sthl,hlv->sthv", context, value_up, preferred_element_type=jnp.float32
    ).astype(jnp.bfloat16)
    attended = attended.reshape(samp_local, step_count, -1)
    partial_terms = jnp.einsum(
        "stk,kd->std",
        lax.all_gather(attended, "grp", axis=0, tiled=True),
        out_weight,
        preferred_element_type=jnp.float32,
    )
    return lax.psum_scatter(
        partial_terms.astype(jnp.bfloat16), "tp", scatter_dimension=0, tiled=True
    )


def solution(mesh):
    return jax.shard_map(
        body,
        mesh=mesh,
        in_specs=(
            P("grp", None, "tp", None),
            P("grp", None, None),
            P(),
            P("grp", None, None),
            P("grp", None, None),
            P("tp", None, None),
            P("tp", None, None),
            P("tp", "grp"),
        ),
        out_specs=P("tp", None, "grp"),
        check_vma=False,
    )
```

profile of v0, /device:TPU:1, one launch (start us, length us, event | category | flops | bytes accessed | tf_op | source)
XLA Modules:
  0.0 658.6 jit_solution(11463970140565258731)
XLA Ops:
  6.5 0.0 copy-start
  6.5 0.0 all-reduce.3.cloned.1.call-start
  7.3 1.1 select_bitcast_fusion.1
  8.5 3.8 select_bitcast_fusion
  12.2 0.0 slice-start.1
  12.2 0.0 copy-start.3
  12.2 0.0 all-reduce.3.cloned.1.call-update
  12.3 0.0 copy-start.2
  12.3 0.0 all-gather.2.cloned.1.call-start
  12.3 1.0 slice-done.1
  13.4 2.9 fusion.19
  16.3 1.6 copy.15
  17.9 0.0 copy-done.3
  17.9 1.2 fusion.40
  19.1 0.0 copy-done.2
  19.1 0.5 fusion.53
  19.6 0.1 reshape.62
  19.7 425.3 %all-reduce.3.cloned.1.call-done = (bf16[8192,512]{1,0:T(8,128)(2,1)}, bf16[64,8192]{1,0:T(8,128)(2,1)}) async-done(((bf16[8192,512]{1,0:T(8,128)(2,1)}, bf16[64,8192]{1,0:T(8,128)(2,1)}), (bf16[8192,512]{1,0:T(8,128)(2,1)}, bf16[64,8192]{1,0:T(8,128)(2,1)})) %all-reduce.3.cloned.1.call-update) | async-done | bytes 9437200 | tf_op jit(solution)/shard_map/psum | solution.py:9
  445.0 0.0 copy-start.1
  445.0 0.0 slice-start
  445.0 17.9 %fusion.54 = f32[1024,8192]{1,0:T(8,128)} fusion(bf16[1024,512]{1,0:T(8,128)(2,1)} %bitcast.71, bf16[8192,512]{1,0:T(8,128)(2,1)} %get-tuple-element.5), kind=kOutput, calls=%fused_computation.49 | convolution fusion | flops 8589934592 | bytes 42991616 | tf_op jit(solution)/shard_map/dot_general | solution.py:30
  462.8 0.0 copy-done.1
  462.8 0.0 slice-done
  462.8 21.2 %fusion.52 = (f32[1024]{0:T(1024)S(1)}, f32[1024,8192]{1,0:T(8,128)}) fusion(f32[1024,8192]{1,0:T(8,128)} %fusion.54, bf16[1024,64]{1,0:T(8,128)(2,1)S(1)} %bitcast.70, bf16[64,8192]{1,0:T(8,128)(2,1)S(1)} %copy-done.1), kind=kOutput, calls=%fused_computation.47 | convolution fusion | flops 1098906624 | bytes 68292608 | tf_op jit(solution)/shard_map/dot_general | solution.py:34
  484.0 0.1 reduce_max.22
  484.1 0.1 fusion.35
  484.2 1.9 fusion.37
  486.1 0.1 reshape.64
  486.2 13.6 %fusion.1 = f32[1024]{0:T(1024)S(1)} fusion(f32[1024,8192]{1,0:T(8,128)} %get-tuple-element.8, f32[1024]{0:T(1024)S(1)} %max.13), kind=kLoop, calls=%fused_computation.3 | loop fusion | flops 16776192 | bytes 33562624 | tf_op jit(solution)/shard_map/reduce_sum | solution.py:56
  499.9 18.3 %fusion.11 = bf16[1024,512]{1,0:T(8,128)(2,1)S(1)} fusion(f32[8,4,32,512]{3,2,1,0:T(8,128)} %fusion.37, bf16[8192,512]{1,0:T(8,128)(2,1)} %get-tuple-element.5, f32[1024,8192]{1,0:T(8,128)} %get-tuple-element.8, f32[1024]{0:T(1024)S(1)} %max.13, f32[1024]{0:T(1024)S(1)} %add.25), kind=kOutput, calls=%fused_computation.14 | convolution fusion | flops 8608284672 | bytes 45096960 | tf_op jit(solution)/shard_map/dot_general | solution.py:57
  518.2 3.1 fusion.28
  521.3 0.8 copy.35
  522.1 0.0 all-gather.2.cloned.1.call-update
  522.1 0.3 reduce-scatter.2.cloned.1.call-start
  522.4 104.6 %all-gather.2.cloned.1.call-done = bf16[256,4,4096]{2,0,1:T(8,128)(2,1)} async-done(((bf16[8,4,4096]{2,0,1:T(8,128)(2,1)}), bf16[256,4,4096]{2,0,1:T(8,128)(2,1)}) %all-gather.2.cloned.1.call-update) | async-done | bytes 8388624 | tf_op jit(solution)/shard_map/all_gather | solution.py:74
  627.0 0.0 copy-done
  627.0 6.6 fusion.22
  633.6 0.0 reduce-scatter.2.cloned.1.call-update
  633.6 16.8 %reduce-scatter.2.cloned.1.call-done = bf16[64,4,224]{2,0,1:T(8,128)(2,1)} async-done(((bf16[256,4,224]{2,0,1:T(8,128)(2,1)}), bf16[64,4,224]{2,0,1:T(8,128)(2,1)}) %reduce-scatter.2.cloned.1.call-update) | async-done | bytes 114704 | tf_op jit(solution)/shard_map/reduce_scatter | solution.py:78
  650.4 1.7 copy.20
  (4 shorter events, 0.0 us)
Async XLA Ops:
  6.5 620.5 %copy-start = (bf16[4096,224]{0,1:T(8,128)(2,1)S(1)}, bf16[4096,224]{0,1:T(8,128)(2,1)}, u32[]{:S(2)}) copy-start(bf16[4096,224]{0,1:T(8,128)(2,1)} %param.15) | copy-start | bytes 5505028
  6.5 438.4 %all-reduce.3.cloned.1.call-start = ((), (), s32[]{:S(2)}) async-start(), calls=%async_computation.3 | async-start | bytes 18874368 | tf_op jit(solution)/shard_map/psum | solution.py:9
  12.2 1.1 slice-start.1
  12.2 5.7 copy-start.3
  12.3 6.9 %copy-start.2 = (bf16[8,4,32,192]{3,2,1,0:T(8,128)(2,1)S(1)}, bf16[8,4,32,192]{3,2,1,0:T(8,128)(2,1)}, u32[]{:S(2)}) copy-start(bf16[8,4,32,192]{3,2,1,0:T(8,128)(2,1)} %param.8) | copy-start | bytes 1179652
  12.3 614.7 %all-gather.2.cloned.1.call-start = ((), (), s32[]{:S(2)}) async-start(), calls=%async_computation.1 | async-start | bytes 8650752 | tf_op jit(solution)/shard_map/all_gather | solution.py:74
  445.0 17.9 %copy-start.1 = (bf16[64,8192]{1,0:T(8,128)(2,1)S(1)}, bf16[64,8192]{1,0:T(8,128)(2,1)}, u32[]{:S(2)}) copy-start(bf16[64,8192]{1,0:T(8,128)(2,1)} %get-tuple-element.6) | copy-start | bytes 3145732
  445.0 17.9 %slice-start = ((bf16[8,4,32,192]{3,2,1,0:T(8,128)(2,1)}), bf16[8,4,32,64]{3,2,1,0:T(8,128)(2,1)S(1)}, s32[]{:S(2)}) async-start(bf16[8,4,32,192]{3,2,1,0:T(8,128)(2,1)} %param.8), calls=%async_computation.4 | async-start | bytes 524288 | tf_op jit(solution)/shard_map/slice | solution.py:23
  522.1 128.3 %reduce-scatter.2.cloned.1.call-start = ((), (), s32[]{:S(2)}) async-start(), calls=%async_computation.2 | async-start | bytes 655360 | tf_op jit(solution)/shard_map/reduce_scatter | solution.py:78
Sparse Core Ops, SparseCore 0:
  12.4 432.5 all-reduce.2
  522.3 104.6 all-gather.1
  633.7 16.6 reduce-scatter.1
where the time goes:
time: 658 us; the launch traced here: 659 us
  waiting for transfers between devices  547 us (83%)
  matrix products  73.6 us (11%)
  other arithmetic  18.7 us (3%)
  between operations  14 us (2%)
    psum x1, waiting for transfers between devices, broadcast(): return lax.psum(jnp.where(mine, x, jnp.zeros_like(x)), axis)  425 us
    all_gather x1, waiting for transfers between devices, body(): lax.all_gather(attended, 'grp', axis=0, tiled=True)  105 us
    dot_general x1, matrix products, body(): jnp.dot(flat_rope, rotary, preferred_element_type=jnp.float32)  21.2 us
    dot_general x1, matrix products, body(): jnp.dot(prefix_exp.astype(jnp.bfloat16), latent, preferred_element_type=j...  18.3 us
    dot_general x1, matrix products, body(): lax.dot_general(flat_latent, latent, (((1,), (1,)), ((), ())), preferred_...  17.9 us
    reduce_scatter x1, waiting for transfers between devices, body(): lax.psum_scatter(partial_terms.astype(jnp.bfloat16), 'tp', scatter_dimens...  16.8 us
    reduce_sum x1, other arithmetic, body(): jnp.sum(prefix_exp, axis=1) + jnp.sum(new_exp, axis=3).reshape(row_count)  13.6 us
  transfers between devices with their start and end apart: 3, of which 3 were waited for; matrix products, arithmetic and copies ran while one was open for 1% of the time, Pallas kernels for 0%

commit v1 on v0

--- a/solution.py
+++ b/solution.py
@@ -1,12 +1,249 @@
+import functools
 import jax
 import jax.numpy as jnp
 from jax import lax
+from jax.experimental import pallas as pl
+from jax.experimental.pallas import tpu as pltpu
 from jax.sharding import PartitionSpec as P
 
-
-def broadcast(x, axis, root):
-    mine = lax.axis_index(axis) == root
-    return lax.psum(jnp.where(mine, x, jnp.zeros_like(x)), axis)
+MESH = pl.DeviceIdType.MESH
+BF = jnp.bfloat16
+
+
+class Coord:
+    def __init__(self):
+        g, t = lax.axis_index("grp"), lax.axis_index("tp")
+        self.x, self.y, self.z, self.c = g // 8, (g // 2) % 4, (g % 2) * 2 + t // 2, t % 2
+
+    def at(self, **moved):
+        x, y, z, c = (moved.get(k, getattr(self, k)) for k in "xyzc")
+        return (x * 8 + y * 2 + z // 2, (z % 2) * 2 + c)
+
+
+ORDERS = (("x", "y", "z"), ("y", "z", "x"), ("z", "x", "y"))
+REGIONS = (
+    (0, "A", 64, 0, 0),
+    (0, "B", 32, 3, 0),
+    (1, "A", 64, 1, 0),
+    (1, "B", 32, 3, 4096),
+    (2, "A", 64, 2, 0),
+    (2, "R", 128, None, None),
+)
+
+
+def source_views(latent):
+    return (
+        latent.reshape(8, 4, 2, 2, 64, 512),
+        latent.reshape(2, 8, 4, 2, 2, 32, 512),
+        latent.reshape(8, 2, 2, 4, 64, 512),
+        latent.reshape(2, 8, 2, 2, 4, 32, 512),
+        latent.reshape(2, 2, 2, 4, 4, 64, 512),
+    )
+
+
+def landing_shapes():
+    shapes = []
+    for lane, kind, unit, _, _ in REGIONS:
+        dims = ((4, 4, 2), (4, 2, 4), (2, 4, 4))[lane]
+        for step in range(3):
+            if kind == "R":
+                width = unit
+                for d in dims[step + 1 :]:
+                    width *= d
+                shapes.append(((dims[step], 32, width), (32, width)))
+            else:
+                tail = dims[step + 1 :] + (unit, 128)
+                shapes.append(((dims[step],) + tail, tail))
+    return shapes
+
+
+def prefix_kernel(owner_ref, v0, v1, v2, v3, v4, rope_ref, lat_ref, rot_ref, *scratch):
+    me = Coord()
+    views = (v0, v1, v2, v3, v4, rope_ref)
+    landings = [(scratch[2 * i], scratch[2 * i + 1]) for i in range(18)]
+    sc_send, sc_recv, sc_own, ag_send, ag_recv, sw_send, sw_recv = scratch[36:]
+    zh, zl = me.z // 2, me.z % 2
+    owner = owner_ref[0]
+    owner_digit = {"x": owner // 8, "y": (owner // 2) % 4, "z": owner % 2}
+
+    barrier = pltpu.get_barrier_semaphore()
+    peers = [me.at(**{a: (getattr(me, a) + d) % 4}) for a in "xyz" for d in (1, 2, 3)]
+    peers.append(me.at(c=1 - me.c))
+    for peer in peers:
+        pl.semaphore_signal(barrier, inc=1, device_id=peer, device_id_type=MESH)
+    pl.semaphore_wait(barrier, len(peers))
+
+    def own_digit(axis):
+        return zh if axis == "z" else getattr(me, axis)
+
+    def source(region, digit):
+        lane, kind, unit, tile, base = REGIONS[region]
+        view = views[region]
+        if kind == "R":
+            start = pl.multiple_of(4096 * digit + 2048 * zl, 128)
+            return view.at[pl.ds(pl.multiple_of(32 * me.c, 32), 32), pl.ds(start, 2048)]
+        cols = pl.ds(tile * 128, 128)
+        if lane == 2:
+            return view.at[me.c, digit, zl, :, :, :, cols]
+        lead = (lane,) if kind == "B" else ()
+        if lane == 0:
+            return view.at[lead + (me.c * 4 + digit, slice(None), slice(None), zl, slice(None), cols)]
+        return view.at[lead + (me.c * 4 + digit, slice(None), zl, slice(None), slice(None), cols)]
+
+    def part(region, step, digit):
+        if step == 0:
+            return source(region, digit)
+        held = landings[region * 3 + step - 1][1]
+        lane, kind, unit, tile, base = REGIONS[region]
+        if kind == "R":
+            width = landings[region * 3 + step][0].shape[2]
+            return held.at[:, pl.ds(pl.multiple_of(digit * width, 128), width)]
+        return held.at[digit]
+
+    def scatter_copies(region, step):
+        axis = ORDERS[REGIONS[region][0]][step]
+        slots = landings[region * 3 + step][0]
+        index = region * 3 + step
+        mine = own_digit(axis)
+        copies = []
+        own = pltpu.make_async_copy(part(region, step, mine), slots.at[mine], sc_own.at[index])
+        for d in (1, 2, 3) if axis != "z" else (2,):
+            if axis == "z":
+                target, digit = (me.z + 2) % 4, 1 - zh
+            else:
+                target = digit = (mine + d) % 4
+            copies.append(
+                pltpu.make_async_remote_copy(
+                    src_ref=part(region, step, digit),
+                    dst_ref=slots.at[mine],
+                    send_sem=sc_send.at[index, d - 1],
+                    recv_sem=sc_recv.at[index, d - 1],
+                    device_id=me.at(**{axis: target}),
+                    device_id_type=MESH,
+                )
+            )
+        return own, copies
+
+    def block(region, level, digits):
+        lane, kind, unit, tile, base = REGIONS[region]
+        count = unit * 4 ** (3 - level)
+        place = 0
+        for k in range(3):
+            place = place * 4 + (digits[k] if k < level else 0)
+        if kind == "R":
+            start = pl.multiple_of(128 * place, 128)
+            return rot_ref.at[pl.ds(pl.multiple_of(32 * me.c, 32), 32), pl.ds(start, count)]
+        start = pl.multiple_of(base + unit * (64 * me.c + place), 32)
+        return lat_ref.at[pl.ds(start, count), pl.ds(tile * 128, 128)]
+
+    order = [ORDERS[r[0]] for r in REGIONS]
+    digits = [tuple(getattr(me, a) for a in o) for o in order]
+    pending = []
+    started = []
+    for region in range(6):
+        own, copies = scatter_copies(region, 0)
+        for copy in copies:
+            copy.start()
+        own.start()
+        started.append((own, copies))
+    for step in range(3):
+        following = []
+        for region in range(6):
+            own, copies = started[region]
+            own.wait()
+            for copy in copies:
+                copy.wait_recv()
+            pending += copies
+            axis = order[region][step]
+            slots, held = landings[region * 3 + step]
+            chosen = slots[owner_digit[axis]]
+            if step < 2:
+                held[...] = chosen
+                own, copies = scatter_copies(region, step + 1)
+                for copy in copies:
+                    copy.start()
+                own.start()
+                following.append((own, copies))
+            else:
+                home = block(region, 3, digits[region])
+                home[...] = chosen
+                following.append(gather_start(region, 3, order, digits, me, block, ag_send, ag_recv))
+        started = following
+
+    swaps = []
+
+    def swap(region, which, first):
+        ref = block(region, 1, (first, 0, 0))
+        copy = pltpu.make_async_remote_copy(
+            src_ref=ref,
+            dst_ref=ref,
+            send_sem=sw_send.at[region, which],
+            recv_sem=sw_recv.at[region, which],
+            device_id=me.at(c=1 - me.c),
+            device_id_type=MESH,
+        )
+        copy.start()
+        swaps.append(copy)
+
+    for level in (3, 2):
+        following = []
+        for region in range(6):
+            for copy in started[region]:
+                copy.wait_recv()
+            pending += started[region]
+            following.append(gather_start(region, level - 1, order, digits, me, block, ag_send, ag_recv))
+            if level == 2:
+                swap(region, 0, digits[region][0])
+        started = following
+    for d in (1, 2, 3):
+        for region in range(6):
+            started[region][d - 1].wait_recv()
+            swap(region, d, (digits[region][0] + 4 - d) % 4)
+    for region in range(6):
+        pending += started[region]
+    for copy in swaps:
+        copy.wait_recv()
+    for copy in pending + swaps:
+        copy.wait_send()
+
+
+def gather_start(region, level, order, digits, me, block, ag_send, ag_recv):
+    axis = order[region][level - 1]
+    ref = block(region, level, digits[region])
+    copies = []
+    for d in (1, 2, 3):
+        copy = pltpu.make_async_remote_copy(
+            src_ref=ref,
+            dst_ref=ref,
+            send_sem=ag_send.at[region, level - 1, d - 1],
+            recv_sem=ag_recv.at[region, level - 1, d - 1],
+            device_id=me.at(**{axis: (getattr(me, axis) + d) % 4}),
+            device_id_type=MESH,
+        )
+        copy.start()
+        copies.append(copy)
+    return copies
+
+
+def gather_prefix(owner_index, latent, rope):
+    scratch = []
+    for slots, held in landing_shapes():
+        scratch += [pltpu.VMEM(slots, BF), pltpu.VMEM(held, BF)]
+    sem = pltpu.SemaphoreType.DMA
+    scratch += [sem((18, 3)), sem((18, 3)), sem((18,)), sem((6, 3, 3)), sem((6, 3, 3)), sem((6, 4)), sem((6, 4))]
+    hbm = pl.BlockSpec(memory_space=pl.ANY)
+    vmem = pl.BlockSpec(memory_space=pltpu.VMEM)
+    return pl.pallas_call(
+        prefix_kernel,
+        out_shape=(jax.ShapeDtypeStruct((8192, 512), BF), jax.ShapeDtypeStruct((64, 8192), BF)),
+        in_specs=[pl.BlockSpec(memory_space=pltpu.SMEM)] + [hbm] * 6,
+        out_specs=(vmem, vmem),
+        scratch_shapes=scratch,
+        compiler_params=pltpu.CompilerParams(
+            collective_id=0, has_side_effects=True, vmem_limit_bytes=48 << 20
+        ),
+        name="gather_prefix",
+    )(owner_index, *source_views(latent), rope)
 
 
 def body(queries, new_kv, owner_index, prefix_latent, prefix_rope, key_up, value_up, out_weight):
@@ -14,11 +251,7 @@
     nope_width = key_up.shape[1]
     latent_width = key_up.shape[2]
     score_scale = query_width ** (-0.5)
-    source_index = owner_index[0]
-    latent, rotary = (
-        broadcast(prefix_latent[0], "grp", source_index),
-        broadcast(prefix_rope[0], "grp", source_index),
-    )
+    latent, rotary = gather_prefix(owner_index, prefix_latent[0], prefix_rope[0])
     q_nope = queries[:, :, :, :nope_width]
     q_rope = queries[:, :, :, nope_width:]
     q_latent = jnp.einsum(

time: 658 us -> 290 us (0.44)
  waiting for transfers between devices: 547 us -> 119 us
  Pallas kernels: 0 us -> 63.7 us
    psum x1 -> x0, waiting for transfers between devices: 425 us -> none  [broadcast(): return lax.psum(jnp.where(mine, x, jnp.zeros_like(x)), axis)]
    pallas_call x0 -> x1, Pallas kernels: none -> 63.7 us  [gather_prefix(): pl.pallas_call(prefix_kernel, out_shape=(jax.ShapeDtypeStruct((8192, 512)...]
  transfers between devices with their start and end apart: 3 -> 2, of which waited for: 3 -> 2; matrix products, arithmetic and copies ran while one was open for 1% -> 0% of each run, Pallas kernels for 0% -> 0%
where the time goes in v1:
time: 290 us
  waiting for transfers between devices  119 us (41%)
  matrix products  73.8 us (25%)
  Pallas kernels  63.7 us (22%)
  between operations  14.1 us (5%)
  other arithmetic  13.8 us (5%)
  local copies, waits for them, and re-layouts  5.38 us (2%)
    all_gather x1, waiting for transfers between devices, body(): lax.all_gather(attended, 'grp', axis=0, tiled=True)  102 us
    pallas_call x1, Pallas kernels, gather_prefix(): pl.pallas_call(prefix_kernel, out_shape=(jax.ShapeDtypeStruct((8192, 512)...  63.7 us
    dot_general x1, matrix products, body(): jnp.dot(flat_rope, rotary, preferred_element_type=jnp.float32)  21.1 us
    dot_general x1, matrix products, body(): jnp.dot(prefix_exp.astype(jnp.bfloat16), latent, preferred_element_type=j...  18.5 us
    dot_general x1, matrix products, body(): lax.dot_general(flat_latent, latent, (((1,), (1,)), ((), ())), preferred_...  17.9 us
    reduce_scatter x1, waiting for transfers between devices, body(): lax.psum_scatter(partial_terms.astype(jnp.bfloat16), 'tp', scatter_dimens...  17 us
    reduce_sum x1, other arithmetic, body(): jnp.sum(prefix_exp, axis=1) + jnp.sum(new_exp, axis=3).reshape(row_count)  13.6 us
    dot_general x1, matrix products, body(): jnp.einsum('stk,kd->std', lax.all_gather(attended, 'grp', axis=0, tiled=T...  6.59 us
  transfers between devices with their start and end apart: 2, of which 2 were waited for; matrix products, arithmetic and copies ran while one was open for 0% of the time, Pallas kernels for 0%

profile of v1, /device:TPU:1, one launch (start us, length us, event | category | flops | bytes accessed | tf_op | source)
XLA Modules:
  0.0 289.6 jit_solution(16943024446651395095)
XLA Ops:
  6.5 0.0 copy-start
  6.5 0.0 copy-start.2
  6.5 0.0 copy-start.4
  6.5 0.0 copy-start.1
  6.5 0.0 all-gather.2.cloned.1.call-start
  6.6 1.1 slice.12
  8.4 2.9 %fusion.19 = bf16[8,4,32,512]{3,0,1,2:T(8,128)(2,1)S(1)} fusion(bf16[32,128,512]{2,1,0:T(8,128)(2,1)} %param.13, bf16[8,4,32,128]{3,2,1,0:T(8,128)(2,1)S(1)} %slice.12), kind=kOutput, calls=%fused_computation.17 | convolution fusion | flops 134742016 | bytes 5505024 | tf_op jit(solution)/shard_map/sthn,hnl->sthl/dot_general | solution.py:257
  11.3 1.6 copy.15
  12.9 0.0 copy-done.4
  12.9 1.2 fusion.40
  14.1 0.0 copy-done.2
  14.1 0.5 fusion.53
  14.6 0.1 reshape.56
  14.7 0.0 copy-done.1
  14.7 0.0 copy-start.3
  14.7 63.7 %gather_prefix.1 = (bf16[8192,512]{1,0:T(8,128)(2,1)}, bf16[64,8192]{1,0:T(8,128)(2,1)S(1)}) custom-call(s32[1]{0:T(128)S(6)} %copy.36.owner_ref, bf16[8,4,2,2,64,512]{5,4,3,2,1,0:T(8,128)(2,1)} %bitcast.71, bf16[2,8,4,2,2,32,512]{6,5,4,3,2,1,0:T(8,128)(2,1)} %bitcast.72, bf16[8,2,2,4,64,512]{5,4,3,2,1,0:T(8,128)(2,1)} %bitcast.73, ...), custom_call_target="tpu_custom_call" | custom-call | tf_op jit(solution)/shard_map/gather_prefix/pallas_call | solution.py:236
  78.3 0.0 copy-done.3
  78.3 0.0 slice-start
  78.4 17.9 %fusion.54 = f32[1024,8192]{1,0:T(8,128)} fusion(bf16[1024,512]{1,0:T(8,128)(2,1)S(1)} %bitcast.77, bf16[8192,512]{1,0:T(8,128)(2,1)} %get-tuple-element.7), kind=kOutput, calls=%fused_computation.47 | convolution fusion | flops 8589934592 | bytes 42991616 | tf_op jit(solution)/shard_map/dot_general | solution.py:263
  96.3 0.0 slice-done
  96.3 21.1 %fusion.52 = (f32[1024]{0:T(1024)S(1)}, f32[1024,8192]{1,0:T(8,128)}) fusion(f32[1024,8192]{1,0:T(8,128)} %fusion.54, bf16[1024,64]{1,0:T(8,128)(2,1)S(1)} %bitcast.76, bf16[64,8192]{1,0:T(8,128)(2,1)S(1)} %get-tuple-element.8), kind=kOutput, calls=%fused_computation.45 | convolution fusion | flops 1098906624 | bytes 68292608 | tf_op jit(solution)/shard_map/dot_general | solution.py:267
  117.4 0.1 reduce_max.22
  117.5 0.1 fusion.35
  117.6 1.9 fusion.37
  119.5 0.1 reshape.58
  119.6 13.6 %fusion.1 = f32[1024]{0:T(1024)S(1)} fusion(f32[1024,8192]{1,0:T(8,128)} %get-tuple-element.10, f32[1024]{0:T(1024)S(1)} %max.13), kind=kLoop, calls=%fused_computation.3 | loop fusion | flops 16776192 | bytes 33562624 | tf_op jit(solution)/shard_map/reduce_sum | solution.py:289
  133.2 18.5 %fusion.11 = bf16[1024,512]{1,0:T(8,128)(2,1)S(1)} fusion(f32[8,4,32,512]{3,2,1,0:T(8,128)} %fusion.37, bf16[8192,512]{1,0:T(8,128)(2,1)} %get-tuple-element.7, f32[1024,8192]{1,0:T(8,128)} %get-tuple-element.10, f32[1024]{0:T(1024)S(1)} %max.13, f32[1024]{0:T(1024)S(1)} %add.21), kind=kOutput, calls=%fused_computation.13 | convolution fusion | flops 8608284672 | bytes 45096960 | tf_op jit(solution)/shard_map/dot_general | solution.py:290
  151.8 3.1 %fusion.28 = bf16[32,4,1,8,128]{4,3,2,1,0:T(8,128)(2,1)S(1)} fusion(bf16[32,512,128]{2,1,0:T(8,128)(2,1)} %param.14, bf16[8,4,32,512]{3,2,1,0:T(8,128)(2,1)S(1)} %bitcast.79), kind=kOutput, calls=%fused_computation.20 | convolution fusion | flops 134348800 | bytes 5505024 | tf_op jit(solution)/shard_map/sthl,hlv->sthv/dot_general | solution.py:301
  154.9 0.8 copy.35
  155.7 0.0 all-gather.2.cloned.1.call-update
  155.7 0.0 reduce-scatter.2.cloned.1.call-start
  155.8 101.7 %all-gather.2.cloned.1.call-done = bf16[256,4,4096]{2,0,1:T(8,128)(2,1)} async-done(((bf16[8,4,4096]{2,0,1:T(8,128)(2,1)}), bf16[256,4,4096]{2,0,1:T(8,128)(2,1)}) %all-gather.2.cloned.1.call-update) | async-done | bytes 8388624 | tf_op jit(solution)/shard_map/all_gather | solution.py:307
  257.5 0.0 copy-done
  257.5 6.6 %fusion.22 = bf16[256,4,224]{2,0,1:T(8,128)(2,1)} fusion(bf16[256,4,4096]{2,0,1:T(8,128)(2,1)} %all-gather.2.cloned.1.call-done, bf16[4096,224]{0,1:T(8,128)(2,1)S(1)} %copy-done), kind=kOutput, calls=%fused_computation.18 | convolution fusion | flops 1879277568 | bytes 10682368 | tf_op jit(solution)/shard_map/stk,kd->std/dot_general | solution.py:305
  264.1 0.0 reduce-scatter.2.cloned.1.call-update
  264.1 17.0 %reduce-scatter.2.cloned.1.call-done = bf16[64,4,224]{2,0,1:T(8,128)(2,1)} async-done(((bf16[256,4,224]{2,0,1:T(8,128)(2,1)}), bf16[64,4,224]{2,0,1:T(8,128)(2,1)}) %reduce-scatter.2.cloned.1.call-update) | async-done | bytes 114704 | tf_op jit(solution)/shard_map/reduce_scatter | solution.py:311
  281.1 1.7 copy.20
  (4 shorter events, 0.0 us)
Async XLA Ops:
  6.5 251.0 %copy-start = (bf16[4096,224]{0,1:T(8,128)(2,1)S(1)}, bf16[4096,224]{0,1:T(8,128)(2,1)}, u32[]{:S(2)}) copy-start(bf16[4096,224]{0,1:T(8,128)(2,1)} %param.15) | copy-start | bytes 5505028
  6.5 7.6 %copy-start.2 = (bf16[8,4,32,192]{3,2,1,0:T(8,128)(2,1)S(1)}, bf16[8,4,32,192]{3,2,1,0:T(8,128)(2,1)}, u32[]{:S(2)}) copy-start(bf16[8,4,32,192]{3,2,1,0:T(8,128)(2,1)} %param.8) | copy-start | bytes 1179652
  6.5 6.3 %copy-start.4 = (bf16[8,4,576]{2,1,0:T(4,128)(2,1)S(1)}, bf16[8,4,576]{2,1,0:T(4,128)(2,1)}, u32[]{:S(2)}) copy-start(bf16[8,4,576]{2,1,0:T(4,128)(2,1)} %param.9) | copy-start | bytes 110596
  6.5 8.1 %copy-start.1 = (bf16[1,64,8192]{2,1,0:T(8,128)(2,1)S(1)}, bf16[1,64,8192]{2,1,0:T(8,128)(2,1)}, u32[]{:S(2)}) copy-start(bf16[1,64,8192]{2,1,0:T(8,128)(2,1)} %param.12) | copy-start | bytes 3145732
  6.5 251.0 %all-gather.2.cloned.1.call-start = ((), (), s32[]{:S(2)}) async-start(), calls=%async_computation.1 | async-start | bytes 8650752 | tf_op jit(solution)/shard_map/all_gather | solution.py:307
  14.7 63.7 %copy-start.3 = (bf16[8,4,32,512]{3,2,1,0:T(8,128)(2,1)S(1)}, bf16[8,4,32,512]{3,2,1,0:T(8,128)(2,1)}, u32[]{:S(2)}) copy-start(bf16[8,4,32,512]{3,2,1,0:T(8,128)(2,1)} %copy.15) | copy-start | bytes 3145732
  78.3 17.9 %slice-start = ((bf16[8,4,32,192]{3,2,1,0:T(8,128)(2,1)}), bf16[8,4,32,64]{3,2,1,0:T(8,128)(2,1)S(1)}, s32[]{:S(2)}) async-start(bf16[8,4,32,192]{3,2,1,0:T(8,128)(2,1)} %param.8), calls=%async_computation.3 | async-start | bytes 524288 | tf_op jit(solution)/shard_map/slice | solution.py:256
  155.7 125.4 %reduce-scatter.2.cloned.1.call-start = ((), (), s32[]{:S(2)}) async-start(), calls=%async_computation.2 | async-start | bytes 655360 | tf_op jit(solution)/shard_map/reduce_scatter | solution.py:311
Sparse Core Ops, SparseCore 0:
  155.8 101.6 all-gather.1
  264.3 16.7 reduce-scatter.1

commit v2 on v1

--- a/solution.py
+++ b/solution.py
@@ -57,11 +57,16 @@
     return shapes
 
 
-def prefix_kernel(owner_ref, v0, v1, v2, v3, v4, rope_ref, lat_ref, rot_ref, *scratch):
+def layer_kernel(
+    owner_ref, q_ref, new_ref, key_hbm, value_hbm, v0, v1, v2, v3, v4, rope_ref, att_ref,
+    lat_ref, rot_ref, key_ref, value_ref, qlat_ref, acc_ref, max_ref, sum_ref, weight_sem, *scratch
+):
     me = Coord()
     views = (v0, v1, v2, v3, v4, rope_ref)
     landings = [(scratch[2 * i], scratch[2 * i + 1]) for i in range(18)]
     sc_send, sc_recv, sc_own, ag_send, ag_recv, sw_send, sw_recv = scratch[36:]
+    key_copy = pltpu.make_async_copy(key_hbm, key_ref, weight_sem.at[0])
+    value_copy = pltpu.make_async_copy(value_hbm, value_ref, weight_sem.at[1])
     zh, zl = me.z // 2, me.z % 2
     owner = owner_ref[0]
     owner_digit = {"x": owner // 8, "y": (owner // 2) % 4, "z": owner % 2}
@@ -146,6 +151,11 @@
             copy.start()
         own.start()
         started.append((own, copies))
+    key_copy.start()
+    value_copy.start()
+    key_copy.wait()
+    latent_queries(q_ref, key_ref, qlat_ref)
+    new_keys(q_ref, new_ref, qlat_ref, acc_ref, max_ref, sum_ref)
     for step in range(3):
         following = []
         for region in range(6):
@@ -206,6 +216,75 @@
     for copy in pending + swaps:
         copy.wait_send()
 
+    prefix_keys(q_ref, qlat_ref, lat_ref, rot_ref, acc_ref, max_ref, sum_ref)
+    value_copy.wait()
+    attended_values(acc_ref, sum_ref, value_ref, att_ref)
+
+
+SCALE = 192**-0.5 * 1.4426950408889634
+LAST = (((1,), (1,)), ((), ()))
+ROWS = 512
+KEYS = 1024
+
+
+def dot(a, b):
+    return jnp.dot(a, b, preferred_element_type=jnp.float32)
+
+
+def dot_last(a, b):
+    return lax.dot_general(a, b, LAST, preferred_element_type=jnp.float32)
+
+
+def latent_queries(q_ref, key_ref, qlat_ref):
+    @pl.loop(0, 32, unroll=4)
+    def _(h):
+        rows = pl.ds(pl.multiple_of(h * 32, 32), 32)
+        qlat_ref[rows, :] = dot(q_ref[rows, 0:128], key_ref[h]).astype(BF)
+
+
+def new_keys(q_ref, new_ref, qlat_ref, acc_ref, max_ref, sum_ref):
+    @pl.loop(0, 1024 // ROWS)
+    def _(r):
+        rows = pl.ds(pl.multiple_of(r * ROWS, ROWS), ROWS)
+        scores = dot_last(qlat_ref[rows, :], new_ref[:, 0:512])
+        scores = (scores + dot_last(q_ref[rows, 128:192], new_ref[:, 512:576])) * SCALE
+        row = lax.broadcasted_iota(jnp.int32, (ROWS, 32), 0) % 32
+        key = lax.broadcasted_iota(jnp.int32, (ROWS, 32), 1)
+        visible = (row // 4 == key // 4) & (key <= row)
+        top = jnp.max(jnp.where(visible, scores, -jnp.inf), axis=1, keepdims=True)
+        e = jnp.where(visible, jnp.exp2(jnp.where(visible, scores, top) - top), 0.0)
+        max_ref[rows, :] = jnp.broadcast_to(top, (ROWS, 128))
+        sum_ref[rows, :] = jnp.broadcast_to(jnp.sum(e, axis=1, keepdims=True), (ROWS, 128))
+        acc_ref[rows, :] = dot(e.astype(BF), new_ref[:, 0:512])
+
+
+def prefix_keys(q_ref, qlat_ref, lat_ref, rot_ref, acc_ref, max_ref, sum_ref):
+    @pl.loop(0, 8192 // KEYS)
+    def _(k):
+        keys = pl.ds(pl.multiple_of(k * KEYS, KEYS), KEYS)
+        blocks = [pl.ds(r * ROWS, ROWS) for r in range(1024 // ROWS)]
+        scores = [
+            dot_last(qlat_ref[rows, :], lat_ref[keys, :]) + dot(q_ref[rows, 128:192], rot_ref[:, keys])
+            for rows in blocks
+        ]
+        for rows, s in zip(blocks, scores):
+            old = max_ref[rows, :]
+            new = jnp.maximum(old, jnp.max(s, axis=1, keepdims=True) * SCALE)
+            max_ref[rows, :] = new
+            shrink = jnp.exp2(old - new)
+            e = jnp.exp2(s * SCALE - new[:, 0:1])
+            sum_ref[rows, :] = sum_ref[rows, :] * shrink + jnp.sum(e, axis=1, keepdims=True)
+            acc_ref[rows, :] = acc_ref[rows, :] * shrink[:, 0:1] + dot(e.astype(BF), lat_ref[keys, :])
+
+
+def attended_values(acc_ref, sum_ref, value_ref, att_ref):
+    @pl.loop(0, 32, unroll=4)
+    def _(h):
+        rows = pl.ds(pl.multiple_of(h * 32, 32), 32)
+        context = (acc_ref[rows, :] / sum_ref[rows, 0:1]).astype(BF)
+        cols = pl.ds(pl.multiple_of(h * 128, 128), 128)
+        att_ref[:, cols] = dot(context, value_ref[h]).astype(BF)
+
 
 def gather_start(region, level, order, digits, me, block, ag_send, ag_recv):
     axis = order[region][level - 1]
@@ -225,8 +304,18 @@
     return copies
 
 
-def gather_prefix(owner_index, latent, rope):
-    scratch = []
+def attend(owner_index, queries, new_kv, key_up, value_up, latent, rope):
+    scratch = [
+        pltpu.VMEM((8192, 512), BF),
+        pltpu.VMEM((64, 8192), BF),
+        pltpu.VMEM((32, 128, 512), BF),
+        pltpu.VMEM((32, 512, 128), BF),
+        pltpu.VMEM((1024, 512), BF),
+        pltpu.VMEM((1024, 512), jnp.float32),
+        pltpu.VMEM((1024, 128), jnp.float32),
+        pltpu.VMEM((1024, 128), jnp.float32),
+        pltpu.SemaphoreType.DMA((2,)),
+    ]
     for slots, held in landing_shapes():
         scratch += [pltpu.VMEM(slots, BF), pltpu.VMEM(held, BF)]
     sem = pltpu.SemaphoreType.DMA
@@ -234,77 +323,27 @@
     hbm = pl.BlockSpec(memory_space=pl.ANY)
     vmem = pl.BlockSpec(memory_space=pltpu.VMEM)
     return pl.pallas_call(
-        prefix_kernel,
-        out_shape=(jax.ShapeDtypeStruct((8192, 512), BF), jax.ShapeDtypeStruct((64, 8192), BF)),
-        in_specs=[pl.BlockSpec(memory_space=pltpu.SMEM)] + [hbm] * 6,
-        out_specs=(vmem, vmem),
+        layer_kernel,
+        out_shape=jax.ShapeDtypeStruct((32, 4096), BF),
+        in_specs=[pl.BlockSpec(memory_space=pltpu.SMEM), vmem, vmem] + [hbm] * 8,
+        out_specs=vmem,
         scratch_shapes=scratch,
         compiler_params=pltpu.CompilerParams(
-            collective_id=0, has_side_effects=True, vmem_limit_bytes=48 << 20
+            collective_id=0, has_side_effects=True, vmem_limit_bytes=60 << 20
         ),
-        name="gather_prefix",
-    )(owner_index, *source_views(latent), rope)
+        name="attend",
+    )(owner_index, queries, new_kv, key_up, value_up, *source_views(latent), rope)
 
 
 def body(queries, new_kv, owner_index, prefix_latent, prefix_rope, key_up, value_up, out_weight):
-    samp_local, step_count, heads_local, query_width = queries.shape
-    nope_width = key_up.shape[1]
-    latent_width = key_up.shape[2]
-    score_scale = query_width ** (-0.5)
-    latent, rotary = gather_prefix(owner_index, prefix_latent[0], prefix_rope[0])
-    q_nope = queries[:, :, :, :nope_width]
-    q_rope = queries[:, :, :, nope_width:]
-    q_latent = jnp.einsum(
-        "sthn,hnl->sthl", q_nope, key_up, preferred_element_type=jnp.float32
-    ).astype(jnp.bfloat16)
-    row_count = samp_local * step_count * heads_local
-    flat_latent = q_latent.reshape(row_count, latent_width)
-    flat_rope = q_rope.reshape(row_count, query_width - nope_width)
-    prefix_scores = lax.dot_general(
-        flat_latent, latent, (((1,), (1,)), ((), ())), preferred_element_type=jnp.float32
-    )
-    prefix_scores = (
-        prefix_scores + jnp.dot(flat_rope, rotary, preferred_element_type=jnp.float32)
-    ) * score_scale
-    new_latent = new_kv[:, :, :latent_width]
-    new_rope = new_kv[:, :, latent_width:]
-    new_scores = jnp.einsum(
-        "sthl,sul->sthu", q_latent, new_latent, preferred_element_type=jnp.float32
-    )
-    new_scores = (
-        new_scores
-        + jnp.einsum("sthr,sur->sthu", q_rope, new_rope, preferred_element_type=jnp.float32)
-    ) * score_scale
-    visible = (jnp.arange(step_count)[None, :] <= jnp.arange(step_count)[:, None])[None, :, None, :]
-    masked = jnp.where(visible, new_scores, -jnp.inf)
-    row_max = jnp.maximum(
-        jnp.max(prefix_scores, axis=1), jnp.max(masked, axis=3).reshape(row_count)
-    )
-    prefix_exp = jnp.exp(prefix_scores - row_max[:, None])
-    new_exp = jnp.where(
-        visible,
-        jnp.exp(masked - row_max.reshape(samp_local, step_count, heads_local)[:, :, :, None]),
-        0.0,
-    )
-    exp_total = jnp.sum(prefix_exp, axis=1) + jnp.sum(new_exp, axis=3).reshape(row_count)
-    context = jnp.dot(prefix_exp.astype(jnp.bfloat16), latent, preferred_element_type=jnp.float32)
-    new_context = jnp.einsum(
-        "sthu,sul->sthl",
-        new_exp.astype(jnp.bfloat16),
-        new_latent,
-        preferred_element_type=jnp.float32,
-    )
-    context = (context + new_context.reshape(row_count, latent_width)) / exp_total[:, None]
-    context = context.astype(jnp.bfloat16).reshape(
-        samp_local, step_count, heads_local, latent_width
-    )
-    attended = jnp.einsum(
-        "sthl,hlv->sthv", context, value_up, preferred_element_type=jnp.float32
-    ).astype(jnp.bfloat16)
-    attended = attended.reshape(samp_local, step_count, -1)
+    samples, steps, heads, width = queries.shape
+    rows = jnp.transpose(queries, (2, 0, 1, 3)).reshape(heads * samples * steps, width)
+    attended = attend(
+        owner_index, rows, new_kv.reshape(samples * steps, -1), key_up, value_up, prefix_latent[0], prefix_rope[0]
+    )
     partial_terms = jnp.einsum(
         "stk,kd->std",
-        lax.all_gather(attended, "grp", axis=0, tiled=True),
+        lax.all_gather(attended.reshape(samples, steps, -1), "grp", axis=0, tiled=True),
         out_weight,
         preferred_element_type=jnp.float32,
     )

time: 290 us -> 236 us (0.81)
  matrix products: 73.8 us -> 6.59 us
  Pallas kernels: 63.7 us -> 89 us
  other arithmetic: 13.8 us -> 0 us
    dot_general x9 -> x1, matrix products: 73.8 us -> 6.59 us  [body(): jnp.einsum('stk,kd->std', lax.all_gather(attended.reshape(samples, steps,...]
    pallas_call x1, Pallas kernels: 63.7 us -> 89 us  [attend(): pl.pallas_call(layer_kernel, out_shape=jax.ShapeDtypeStruct((32, 4096), B...]
    reduce_sum x2 -> x0, other arithmetic: 13.8 us -> none  [the longest x1 13.6 us: body(): jnp.sum(prefix_exp, axis=1) + jnp.sum(new_exp, axis=3).reshape(row_count)]
    reshape x3 -> x4, local copies, waits for them, and re-layouts: 0.93 us -> 4.46 us  [the longest x2 1.92 us: body(): attended.reshape(samples, steps, -1)]
where the time goes in v2:
time: 236 us
  waiting for transfers between devices  119 us (50%)
  Pallas kernels  89 us (38%)
  between operations  14.2 us (6%)
  local copies, waits for them, and re-layouts  7.58 us (3%)
  matrix products  6.59 us (3%)
    all_gather x1, waiting for transfers between devices, body(): lax.all_gather(attended.reshape(samples, steps, -1), 'grp', axis=0, tiled...  102 us
    pallas_call x1, Pallas kernels, attend(): pl.pallas_call(layer_kernel, out_shape=jax.ShapeDtypeStruct((32, 4096), B...  89 us
    reduce_scatter x1, waiting for transfers between devices, body(): lax.psum_scatter(partial_terms.astype(jnp.bfloat16), 'tp', scatter_dimens...  17 us
    dot_general x1, matrix products, body(): jnp.einsum('stk,kd->std', lax.all_gather(attended.reshape(samples, steps,...  6.59 us
  transfers between devices with their start and end apart: 2, of which 2 were waited for; matrix products, arithmetic and copies ran while one was open for 0% of the time, Pallas kernels for 0%

profile of v2, /device:TPU:1, one launch (start us, length us, event | category | flops | bytes accessed | tf_op | source)
XLA Modules:
  0.0 236.2 jit_solution(3950187105731460198)
XLA Ops:
  6.5 0.0 copy-start
  6.5 0.0 all-gather.2.cloned.1.call-start
  7.3 1.4 reshape.10.new_ref
  8.7 1.4 copy.12
  10.2 1.1 reshape.9.q_ref
  11.3 89.0 %attend.1 = bf16[32,4096]{1,0:T(8,128)(2,1)} custom-call(s32[1]{0:T(128)S(6)} %copy.15.owner_ref, bf16[1024,192]{1,0:T(8,128)(2,1)} %reshape.9.q_ref, bf16[32,576]{1,0:T(8,128)(2,1)} %reshape.10.new_ref, bf16[32,128,512]{2,1,0:T(8,128)(2,1)} %key_hbm.1, bf16[32,512,128]{2,1,0:T(8,128)(2,1)} %value_hbm.1, bf16[8,4,2,2,64,512]{5,4,3,2,1,0:T(8,128)(2,1)} %bitcast.13, ...), custom_call_target="tpu_custom_call" | custom-call | tf_op jit(solution)/shard_map/attend/pallas_call | solution.py:325
  100.3 1.1 reshape.11
  101.4 0.9 copy.13
  102.2 0.0 all-gather.2.cloned.1.call-update
  102.3 0.0 reduce-scatter.2.cloned.1.call-start
  102.3 101.8 %all-gather.2.cloned.1.call-done = bf16[256,4,4096]{2,0,1:T(8,128)(2,1)} async-done(((bf16[8,4,4096]{2,0,1:T(8,128)(2,1)}), bf16[256,4,4096]{2,0,1:T(8,128)(2,1)}) %all-gather.2.cloned.1.call-update) | async-done | bytes 8388624 | tf_op jit(solution)/shard_map/all_gather | solution.py:346
  204.1 0.0 copy-done
  204.1 6.6 %fusion.2 = bf16[256,4,224]{2,0,1:T(8,128)(2,1)} fusion(bf16[256,4,4096]{2,0,1:T(8,128)(2,1)} %all-gather.2.cloned.1.call-done, bf16[4096,224]{0,1:T(8,128)(2,1)S(1)} %copy-done), kind=kOutput, calls=%fused_computation.2 | convolution fusion | flops 1879277568 | bytes 10682368 | tf_op jit(solution)/shard_map/stk,kd->std/dot_general | solution.py:344
  210.7 0.0 reduce-scatter.2.cloned.1.call-update
  210.7 17.0 %reduce-scatter.2.cloned.1.call-done = bf16[64,4,224]{2,0,1:T(8,128)(2,1)} async-done(((bf16[256,4,224]{2,0,1:T(8,128)(2,1)}), bf16[64,4,224]{2,0,1:T(8,128)(2,1)}) %reduce-scatter.2.cloned.1.call-update) | async-done | bytes 114704 | tf_op jit(solution)/shard_map/reduce_scatter | solution.py:350
  227.7 1.7 copy.14
Async XLA Ops:
  6.5 197.6 %copy-start = (bf16[4096,224]{0,1:T(8,128)(2,1)S(1)}, bf16[4096,224]{0,1:T(8,128)(2,1)}, u32[]{:S(2)}) copy-start(bf16[4096,224]{0,1:T(8,128)(2,1)} %param.15) | copy-start | bytes 5505028
  6.5 197.5 %all-gather.2.cloned.1.call-start = ((), (), s32[]{:S(2)}) async-start(), calls=%async_computation.1 | async-start | bytes 8650752 | tf_op jit(solution)/shard_map/all_gather | solution.py:346
  102.3 125.4 %reduce-scatter.2.cloned.1.call-start = ((), (), s32[]{:S(2)}) async-start(), calls=%async_computation.2 | async-start | bytes 655360 | tf_op jit(solution)/shard_map/reduce_scatter | solution.py:350
Sparse Core Ops, SparseCore 0:
  102.4 101.6 all-gather.1
  210.8 16.7 reduce-scatter.1

commit v3 on v2

--- a/solution.py
+++ b/solution.py
@@ -58,8 +58,9 @@
 
 
 def layer_kernel(
-    owner_ref, q_ref, new_ref, key_hbm, value_hbm, v0, v1, v2, v3, v4, rope_ref, att_ref,
-    lat_ref, rot_ref, key_ref, value_ref, qlat_ref, acc_ref, max_ref, sum_ref, weight_sem, *scratch
+    owner_ref, q_ref, new_ref, key_hbm, value_hbm, weight_hbm, v0, v1, v2, v3, v4, rope_ref, out_ref,
+    lat_ref, rot_ref, key_ref, value_ref, weight_ref, qlat_ref, score_ref, acc_ref, max_ref, sum_ref,
+    att_ref, total_ref, part_ref, weight_sem, ex_send, ex_recv, rs_send, rs_recv, *scratch
 ):
     me = Coord()
     views = (v0, v1, v2, v3, v4, rope_ref)
@@ -67,13 +68,15 @@
     sc_send, sc_recv, sc_own, ag_send, ag_recv, sw_send, sw_recv = scratch[36:]
     key_copy = pltpu.make_async_copy(key_hbm, key_ref, weight_sem.at[0])
     value_copy = pltpu.make_async_copy(value_hbm, value_ref, weight_sem.at[1])
+    weight_copy = pltpu.make_async_copy(weight_hbm, weight_ref, weight_sem.at[2])
     zh, zl = me.z // 2, me.z % 2
     owner = owner_ref[0]
     owner_digit = {"x": owner // 8, "y": (owner // 2) % 4, "z": owner % 2}
 
     barrier = pltpu.get_barrier_semaphore()
     peers = [me.at(**{a: (getattr(me, a) + d) % 4}) for a in "xyz" for d in (1, 2, 3)]
-    peers.append(me.at(c=1 - me.c))
+    z_mate = me.z + 1 - 2 * zl
+    peers += [me.at(c=1 - me.c), me.at(z=z_mate, c=1 - me.c)]
     for peer in peers:
         pl.semaphore_signal(barrier, inc=1, device_id=peer, device_id_type=MESH)
     pl.semaphore_wait(barrier, len(peers))
@@ -153,6 +156,7 @@
         started.append((own, copies))
     key_copy.start()
     value_copy.start()
+    weight_copy.start()
     key_copy.wait()
     latent_queries(q_ref, key_ref, qlat_ref)
     new_keys(q_ref, new_ref, qlat_ref, acc_ref, max_ref, sum_ref)
@@ -213,17 +217,103 @@
         pending += started[region]
     for copy in swaps:
         copy.wait_recv()
-    for copy in pending + swaps:
+    pending += swaps
+
+    def exchange(chunk):
+        for step in range(3):
+            copies = []
+            for lane, (low, high) in enumerate(EX_LANES):
+                axis = EX_ORDERS[lane][step]
+                done = EX_ORDERS[lane][:step]
+                cols = pl.ds(chunk * CHUNK + low, high - low)
+                where = tuple(
+                    slice(None) if a in done else d for a, d in (("x", me.x), ("y", me.y), ("z", zh))
+                )
+                ref = att_ref.at[where + (slice(None), cols)]
+                for d in (1, 2, 3) if axis != "z" else (2,):
+                    copy = pltpu.make_async_remote_copy(
+                        src_ref=ref,
+                        dst_ref=ref,
+                        send_sem=ex_send.at[chunk, lane * 3 + step, d - 1],
+                        recv_sem=ex_recv.at[chunk, lane * 3 + step, d - 1],
+                        device_id=me.at(**{axis: (getattr(me, axis) + d) % 4}),
+                        device_id_type=MESH,
+                    )
+                    copy.start()
+                    copies.append(copy)
+            yield
+            for copy in copies:
+                copy.wait_recv()
+            pending.extend(copies)
+
+    def partial_out(chunk, block):
+        cols = pl.ds(chunk * CHUNK, CHUNK)
+        values = att_ref[block, :, :, :, cols].reshape(256, CHUNK)
+        return dot_last(values, weight_ref[:, cols])
+
+    active = []
+    for chunk in range(CHUNKS):
+        for piece in range(2):
+            prefix_keys(chunk * ROWS, piece * 4, 4, q_ref, qlat_ref, lat_ref, rot_ref, score_ref, acc_ref, max_ref, sum_ref)
+            for steps in active:
+                if steps[0] < 3:
+                    next(steps[1])
+                    steps[0] += 1
+        if chunk == 0:
+            value_copy.wait()
+        attended_values(chunk, acc_ref, sum_ref, value_ref, att_ref, (me.x, me.y, zh))
+        active.append([1, exchange(chunk)])
+        next(active[-1][1])
+    weight_copy.wait()
+    for chunk in range(CHUNKS - 1):
+        for steps in active[chunk:]:
+            if steps[0] < 3 and steps is not active[chunk]:
+                next(steps[1])
+                steps[0] += 1
+        for _ in active[chunk][1]:
+            pass
+        @pl.loop(0, 4)
+        def _(block):
+            term = partial_out(chunk, block)
+            total_ref[block] = term if chunk == 0 else total_ref[block] + term
+    for _ in active[-1][1]:
+        pass
+    tp = zl * 2 + me.c
+    for d, (flip_z, flip_c) in enumerate(((1, 1), (1, 0), (0, 1), (0, 0))):
+        target_z = z_mate if flip_z else me.z
+        target_c = 1 - me.c if flip_c else me.c
+        block = (target_z % 2) * 2 + target_c
+        term = total_ref[block] + partial_out(CHUNKS - 1, block)
+        if d == 3:
+            total_ref[block] = term
+            continue
+        part_ref[d] = term.astype(BF)
+        copy = pltpu.make_async_remote_copy(
+            src_ref=part_ref.at[d],
+            dst_ref=part_ref.at[3 + d],
+            send_sem=rs_send.at[d],
+            recv_sem=rs_recv.at[d],
+            device_id=me.at(z=target_z, c=target_c),
+            device_id_type=MESH,
+        )
+        copy.start()
+        pending.append(copy)
+    result = total_ref[tp]
+    for d, copy in enumerate(pending[-3:]):
+        copy.wait_recv()
+        result = result + part_ref[3 + d].astype(jnp.float32)
+    out_ref[...] = result.astype(BF)
+    for copy in pending:
         copy.wait_send()
 
-    prefix_keys(q_ref, qlat_ref, lat_ref, rot_ref, acc_ref, max_ref, sum_ref)
-    value_copy.wait()
-    attended_values(acc_ref, sum_ref, value_ref, att_ref)
-
-
+
+CHUNKS = 4
+CHUNK = 4096 // CHUNKS
+EX_ORDERS = (("z", "y", "x"), ("x", "z", "y"), ("y", "x", "z"))
+EX_LANES = ((0, 256), (256, 640), (640, 1024))
 SCALE = 192**-0.5 * 1.4426950408889634
 LAST = (((1,), (1,)), ((), ()))
-ROWS = 512
+ROWS = 1024 // CHUNKS
 KEYS = 1024
 
 
@@ -258,32 +348,46 @@
         acc_ref[rows, :] = dot(e.astype(BF), new_ref[:, 0:512])
 
 
-def prefix_keys(q_ref, qlat_ref, lat_ref, rot_ref, acc_ref, max_ref, sum_ref):
-    @pl.loop(0, 8192 // KEYS)
-    def _(k):
+def prefix_keys(row, first, count, q_ref, qlat_ref, lat_ref, rot_ref, score_ref, acc_ref, max_ref, sum_ref):
+    rows = pl.ds(row, ROWS)
+
+    def scores(k):
         keys = pl.ds(pl.multiple_of(k * KEYS, KEYS), KEYS)
-        blocks = [pl.ds(r * ROWS, ROWS) for r in range(1024 // ROWS)]
-        scores = [
-            dot_last(qlat_ref[rows, :], lat_ref[keys, :]) + dot(q_ref[rows, 128:192], rot_ref[:, keys])
-            for rows in blocks
-        ]
-        for rows, s in zip(blocks, scores):
-            old = max_ref[rows, :]
-            new = jnp.maximum(old, jnp.max(s, axis=1, keepdims=True) * SCALE)
-            max_ref[rows, :] = new
-            shrink = jnp.exp2(old - new)
-            e = jnp.exp2(s * SCALE - new[:, 0:1])
-            sum_ref[rows, :] = sum_ref[rows, :] * shrink + jnp.sum(e, axis=1, keepdims=True)
-            acc_ref[rows, :] = acc_ref[rows, :] * shrink[:, 0:1] + dot(e.astype(BF), lat_ref[keys, :])
-
-
-def attended_values(acc_ref, sum_ref, value_ref, att_ref):
-    @pl.loop(0, 32, unroll=4)
+        return dot_last(qlat_ref[rows, :], lat_ref[keys, :]) + dot(q_ref[rows, 128:192], rot_ref[:, keys])
+
+    def take(k, s):
+        keys = pl.ds(pl.multiple_of(k * KEYS, KEYS), KEYS)
+        old = max_ref[rows, :]
+        new = jnp.maximum(old, jnp.max(s, axis=1, keepdims=True) * SCALE)
+        max_ref[rows, :] = new
+        shrink = jnp.exp2(old - new)
+        e = jnp.exp2(s * SCALE - new[:, 0:1])
+        sum_ref[rows, :] = sum_ref[rows, :] * shrink + jnp.sum(e, axis=1, keepdims=True)
+        acc_ref[rows, :] = acc_ref[rows, :] * shrink[:, 0:1] + dot(e.astype(BF), lat_ref[keys, :])
+
+    if first == 0:
+        score_ref[0] = scores(0)
+
+    @pl.loop(first // 2, (first + count) // 2)
+    def _(pair):
+        k = pair * 2
+        s = score_ref[0]
+        score_ref[1] = scores(k + 1)
+        take(k, s)
+        s = score_ref[1]
+        score_ref[0] = scores(jnp.minimum(k + 2, 8192 // KEYS - 1))
+        take(k + 1, s)
+
+
+def attended_values(chunk, acc_ref, sum_ref, value_ref, att_ref, place):
+    heads = 32 // CHUNKS
+
+    @pl.loop(chunk * heads, (chunk + 1) * heads, unroll=4)
     def _(h):
         rows = pl.ds(pl.multiple_of(h * 32, 32), 32)
         context = (acc_ref[rows, :] / sum_ref[rows, 0:1]).astype(BF)
         cols = pl.ds(pl.multiple_of(h * 128, 128), 128)
-        att_ref[:, cols] = dot(context, value_ref[h]).astype(BF)
+        att_ref[place + (slice(None), cols)] = dot(context, value_ref[h]).astype(BF)
 
 
 def gather_start(region, level, order, digits, me, block, ag_send, ag_recv):
@@ -304,52 +408,54 @@
     return copies
 
 
-def attend(owner_index, queries, new_kv, key_up, value_up, latent, rope):
+def layer(owner_index, queries, new_kv, key_up, value_up, out_weight, latent, rope):
+    sem = pltpu.SemaphoreType.DMA
+    f32 = jnp.float32
     scratch = [
         pltpu.VMEM((8192, 512), BF),
         pltpu.VMEM((64, 8192), BF),
         pltpu.VMEM((32, 128, 512), BF),
         pltpu.VMEM((32, 512, 128), BF),
+        pltpu.VMEM((224, 4096), BF),
         pltpu.VMEM((1024, 512), BF),
-        pltpu.VMEM((1024, 512), jnp.float32),
-        pltpu.VMEM((1024, 128), jnp.float32),
-        pltpu.VMEM((1024, 128), jnp.float32),
-        pltpu.SemaphoreType.DMA((2,)),
+        pltpu.VMEM((2, ROWS, KEYS), f32),
+        pltpu.VMEM((1024, 512), f32),
+        pltpu.VMEM((1024, 128), f32),
+        pltpu.VMEM((1024, 128), f32),
+        pltpu.VMEM((4, 4, 2, 32, 4096), BF),
+        pltpu.VMEM((4, 256, 224), f32),
+        pltpu.VMEM((6, 256, 224), BF),
+        sem((3,)),
+        sem((CHUNKS, 9, 3)),
+        sem((CHUNKS, 9, 3)),
+        sem((3,)),
+        sem((3,)),
     ]
     for slots, held in landing_shapes():
         scratch += [pltpu.VMEM(slots, BF), pltpu.VMEM(held, BF)]
-    sem = pltpu.SemaphoreType.DMA
     scratch += [sem((18, 3)), sem((18, 3)), sem((18,)), sem((6, 3, 3)), sem((6, 3, 3)), sem((6, 4)), sem((6, 4))]
     hbm = pl.BlockSpec(memory_space=pl.ANY)
     vmem = pl.BlockSpec(memory_space=pltpu.VMEM)
     return pl.pallas_call(
         layer_kernel,
-        out_shape=jax.ShapeDtypeStruct((32, 4096), BF),
-        in_specs=[pl.BlockSpec(memory_space=pltpu.SMEM), vmem, vmem] + [hbm] * 8,
+        out_shape=jax.ShapeDtypeStruct((256, 224), BF),
+        in_specs=[pl.BlockSpec(memory_space=pltpu.SMEM), vmem, vmem] + [hbm] * 9,
         out_specs=vmem,
         scratch_shapes=scratch,
         compiler_params=pltpu.CompilerParams(
             collective_id=0, has_side_effects=True, vmem_limit_bytes=60 << 20
         ),
-        name="attend",
-    )(owner_index, queries, new_kv, key_up, value_up, *source_views(latent), rope)
+        name="layer",
+    )(owner_index, queries, new_kv, key_up, value_up, out_weight, *source_views(latent), rope)
 
 
 def body(queries, new_kv, owner_index, prefix_latent, prefix_rope, key_up, value_up, out_weight):
     samples, steps, heads, width = queries.shape
-    rows = jnp.transpose(queries, (2, 0, 1, 3)).reshape(heads * samples * steps, width)
-    attended = attend(
-        owner_index, rows, new_kv.reshape(samples * steps, -1), key_up, value_up, prefix_latent[0], prefix_rope[0]
+    rows = jnp.transpose(queries.reshape(samples * steps, heads, width), (1, 0, 2)).reshape(-1, width)
+    out = layer(
+        owner_index, rows, new_kv.reshape(samples * steps, -1), key_up, value_up, out_weight.T, prefix_latent[0], prefix_rope[0]
     )
-    partial_terms = jnp.einsum(
-        "stk,kd->std",
-        lax.all_gather(attended.reshape(samples, steps, -1), "grp", axis=0, tiled=True),
-        out_weight,
-        preferred_element_type=jnp.float32,
-    )
-    return lax.psum_scatter(
-        partial_terms.astype(jnp.bfloat16), "tp", scatter_dimension=0, tiled=True
-    )
+    return out.reshape(64, steps, -1)
 
 
 def solution(mesh):

time: 236 us -> 156 us (0.66); the launches traced: 236 us -> 153 us
  waiting for transfers between devices: 119 us -> 0 us
  Pallas kernels: 89 us -> 147 us
  between operations: 14.2 us -> 0.66 us
  matrix products: 6.59 us -> 0 us
  local copies, waits for them, and re-layouts: 7.58 us -> 5.15 us
    all_gather x1 -> x0, waiting for transfers between devices: 102 us -> none  [body(): lax.all_gather(attended.reshape(samples, steps, -1), 'grp', axis=0, tiled...]
    pallas_call x1, Pallas kernels: 89 us -> 147 us  [layer(): pl.pallas_call(layer_kernel, out_shape=jax.ShapeDtypeStruct((256, 224), B...]
    reduce_scatter x1 -> x0, waiting for transfers between devices: 17 us -> none  [body(): lax.psum_scatter(partial_terms.astype(jnp.bfloat16), 'tp', scatter_dimens...]
    dot_general x1 -> x0, matrix products: 6.59 us -> none  [body(): jnp.einsum('stk,kd->std', lax.all_gather(attended.reshape(samples, steps,...]
  transfers between devices with their start and end apart: 2 -> 0, of which waited for: 2 -> 0; matrix products, arithmetic and copies ran while one was open for 0% -> 0% of each run, Pallas kernels for 0% -> 0%
where the time goes in v3:
time: 156 us; the launch traced here: 153 us
  Pallas kernels  147 us (94%)
  local copies, waits for them, and re-layouts  5.15 us (3%)
    pallas_call x1, Pallas kernels, layer(): pl.pallas_call(layer_kernel, out_shape=jax.ShapeDtypeStruct((256, 224), B...  147 us

profile of v3, /device:TPU:1, one launch (start us, length us, event | category | flops | bytes accessed | tf_op | source)
XLA Modules:
  0.0 153.3 jit_solution(18413621247349316740)
XLA Ops:
  0.7 1.4 reshape.14.new_ref
  2.1 2.1 %copy.10 = bf16[32,32,192]{2,0,1:T(8,128)(2,1)} copy(bf16[32,32,192]{2,1,0:T(8,128)(2,1)} %bitcast.19) | data formatting | bytes 786432 | tf_op jit(solution)/shard_map/reshape | solution.py:454
  4.2 147.5 %layer.1 = bf16[256,224]{1,0:T(8,128)(2,1)} custom-call(s32[1]{0:T(128)S(6)} %copy.11.owner_ref, bf16[1024,192]{1,0:T(8,128)(2,1)} %bitcast.16, bf16[32,576]{1,0:T(8,128)(2,1)} %reshape.14.new_ref, bf16[32,128,512]{2,1,0:T(8,128)(2,1)} %key_hbm.1, bf16[32,512,128]{2,1,0:T(8,128)(2,1)} %value_hbm.1, bf16[224,4096]{1,0:T(8,128)(2,1)} %bitcast.17, ...), custom_call_target="tpu_custom_call" | custom-call | tf_op jit(solution)/shard_map/layer/pallas_call | solution.py:439
  151.7 1.6 %reshape.15 = bf16[64,4,224]{2,1,0:T(4,128)(2,1)} reshape(bf16[256,224]{1,0:T(8,128)(2,1)} %layer.1) | data formatting | bytes 229376 | tf_op jit(solution)/shard_map/reshape | solution.py:458

commit v4 on v3

--- a/solution.py
+++ b/solution.py
@@ -60,7 +60,7 @@
 def layer_kernel(
     owner_ref, q_ref, new_ref, key_hbm, value_hbm, weight_hbm, v0, v1, v2, v3, v4, rope_ref, out_ref,
     lat_ref, rot_ref, key_ref, value_ref, weight_ref, qlat_ref, score_ref, acc_ref, max_ref, sum_ref,
-    att_ref, total_ref, part_ref, weight_sem, ex_send, ex_recv, rs_send, rs_recv, *scratch
+    att_ref, total_ref, part_ref, land_ref, weight_sem, ex_send, ex_recv, rs_send, rs_recv, *scratch
 ):
     me = Coord()
     views = (v0, v1, v2, v3, v4, rope_ref)
@@ -68,15 +68,22 @@
     sc_send, sc_recv, sc_own, ag_send, ag_recv, sw_send, sw_recv = scratch[36:]
     key_copy = pltpu.make_async_copy(key_hbm, key_ref, weight_sem.at[0])
     value_copy = pltpu.make_async_copy(value_hbm, value_ref, weight_sem.at[1])
-    weight_copy = pltpu.make_async_copy(weight_hbm, weight_ref, weight_sem.at[2])
     zh, zl = me.z // 2, me.z % 2
+    weight_copy = pltpu.make_async_copy(weight_hbm, weight_ref.at[zh], weight_sem.at[2])
+    weight_send = pltpu.make_async_remote_copy(
+        src_ref=weight_hbm,
+        dst_ref=weight_ref.at[zh],
+        send_sem=weight_sem.at[3],
+        recv_sem=weight_sem.at[4],
+        device_id=me.at(z=(me.z + 2) % 4),
+        device_id_type=MESH,
+    )
     owner = owner_ref[0]
     owner_digit = {"x": owner // 8, "y": (owner // 2) % 4, "z": owner % 2}
 
     barrier = pltpu.get_barrier_semaphore()
     peers = [me.at(**{a: (getattr(me, a) + d) % 4}) for a in "xyz" for d in (1, 2, 3)]
-    z_mate = me.z + 1 - 2 * zl
-    peers += [me.at(c=1 - me.c), me.at(z=z_mate, c=1 - me.c)]
+    peers += [me.at(z=(me.z + d) % 4, c=1 - me.c) for d in range(4)]
     for peer in peers:
         pl.semaphore_signal(barrier, inc=1, device_id=peer, device_id_type=MESH)
     pl.semaphore_wait(barrier, len(peers))
@@ -219,23 +226,23 @@
         copy.wait_recv()
     pending += swaps
 
+    weight_send.start()
+
     def exchange(chunk):
-        for step in range(3):
+        for step in range(2):
             copies = []
             for lane, (low, high) in enumerate(EX_LANES):
                 axis = EX_ORDERS[lane][step]
                 done = EX_ORDERS[lane][:step]
                 cols = pl.ds(chunk * CHUNK + low, high - low)
-                where = tuple(
-                    slice(None) if a in done else d for a, d in (("x", me.x), ("y", me.y), ("z", zh))
-                )
+                where = tuple(slice(None) if a in done else getattr(me, a) for a in "xy")
                 ref = att_ref.at[where + (slice(None), cols)]
-                for d in (1, 2, 3) if axis != "z" else (2,):
+                for d in (1, 2, 3):
                     copy = pltpu.make_async_remote_copy(
                         src_ref=ref,
                         dst_ref=ref,
-                        send_sem=ex_send.at[chunk, lane * 3 + step, d - 1],
-                        recv_sem=ex_recv.at[chunk, lane * 3 + step, d - 1],
+                        send_sem=ex_send.at[chunk, lane * 2 + step, d - 1],
+                        recv_sem=ex_recv.at[chunk, lane * 2 + step, d - 1],
                         device_id=me.at(**{axis: (getattr(me, axis) + d) % 4}),
                         device_id_type=MESH,
                     )
@@ -246,71 +253,76 @@
                 copy.wait_recv()
             pending.extend(copies)
 
-    def partial_out(chunk, block):
+    def partial_out(chunk, half):
         cols = pl.ds(chunk * CHUNK, CHUNK)
-        values = att_ref[block, :, :, :, cols].reshape(256, CHUNK)
-        return dot_last(values, weight_ref[:, cols])
+        values = att_ref[:, :, :, cols].reshape(512, CHUNK)
+        return dot_last(values, weight_ref[half, :, cols])
 
     active = []
     for chunk in range(CHUNKS):
         for piece in range(2):
             prefix_keys(chunk * ROWS, piece * 4, 4, q_ref, qlat_ref, lat_ref, rot_ref, score_ref, acc_ref, max_ref, sum_ref)
-            for steps in active:
-                if steps[0] < 3:
-                    next(steps[1])
-                    steps[0] += 1
+            if active and piece == 0:
+                next(active[-1])
         if chunk == 0:
             value_copy.wait()
-        attended_values(chunk, acc_ref, sum_ref, value_ref, att_ref, (me.x, me.y, zh))
-        active.append([1, exchange(chunk)])
-        next(active[-1][1])
+        attended_values(chunk, acc_ref, sum_ref, value_ref, att_ref, (me.x, me.y))
+        active.append(exchange(chunk))
+        next(active[-1])
     weight_copy.wait()
     for chunk in range(CHUNKS - 1):
-        for steps in active[chunk:]:
-            if steps[0] < 3 and steps is not active[chunk]:
-                next(steps[1])
-                steps[0] += 1
-        for _ in active[chunk][1]:
+        for _ in active[chunk]:
             pass
-        @pl.loop(0, 4)
-        def _(block):
-            term = partial_out(chunk, block)
-            total_ref[block] = term if chunk == 0 else total_ref[block] + term
-    for _ in active[-1][1]:
+        if chunk == 0:
+            next(active[-1])
+            weight_send.wait_recv()
+
+        @pl.loop(0, 2)
+        def _(half):
+            term = partial_out(chunk, half)
+            total_ref[half] = term if chunk == 0 else total_ref[half] + term
+    for _ in active[-1]:
         pass
-    tp = zl * 2 + me.c
-    for d, (flip_z, flip_c) in enumerate(((1, 1), (1, 0), (0, 1), (0, 0))):
-        target_z = z_mate if flip_z else me.z
-        target_c = 1 - me.c if flip_c else me.c
-        block = (target_z % 2) * 2 + target_c
-        term = total_ref[block] + partial_out(CHUNKS - 1, block)
-        if d == 3:
-            total_ref[block] = term
-            continue
-        part_ref[d] = term.astype(BF)
-        copy = pltpu.make_async_remote_copy(
-            src_ref=part_ref.at[d],
-            dst_ref=part_ref.at[3 + d],
-            send_sem=rs_send.at[d],
-            recv_sem=rs_recv.at[d],
-            device_id=me.at(z=target_z, c=target_c),
-            device_id_type=MESH,
-        )
-        copy.start()
-        pending.append(copy)
-    result = total_ref[tp]
-    for d, copy in enumerate(pending[-3:]):
+    sends = []
+    for far in (1, 0):
+        half = 1 - zh if far else zh
+        total_ref[half] = total_ref[half] + partial_out(CHUNKS - 1, half)
+        for flip_z in (1, 0):
+            for flip_c in (1, 0):
+                target_l = 1 - zl if flip_z else zl
+                target_c = 1 - me.c if flip_c else me.c
+                slot = 4 * far + 2 * flip_z + flip_c
+                if slot == 0:
+                    continue
+                rows = pl.ds(pl.multiple_of((target_l * 2 + target_c) * 128, 128), 128)
+                part_ref[slot] = total_ref[half, rows, :].astype(BF)
+                copy = pltpu.make_async_remote_copy(
+                    src_ref=part_ref.at[slot],
+                    dst_ref=land_ref.at[slot],
+                    send_sem=rs_send.at[slot],
+                    recv_sem=rs_recv.at[slot],
+                    device_id=me.at(z=half * 2 + target_l, c=target_c),
+                    device_id_type=MESH,
+                )
+                copy.start()
+                sends.append(copy)
+    for copy in sends:
         copy.wait_recv()
-        result = result + part_ref[3 + d].astype(jnp.float32)
-    out_ref[...] = result.astype(BF)
-    for copy in pending:
+    own_rows = pl.ds(pl.multiple_of((zl * 2 + me.c) * 128, 128), 128)
+    for far in (0, 1):
+        result = land_ref[4 * far + 1].astype(jnp.float32) + land_ref[4 * far + 2].astype(jnp.float32)
+        result = result + land_ref[4 * far + 3].astype(jnp.float32)
+        result = result + (land_ref[4].astype(jnp.float32) if far else total_ref[zh, own_rows, :])
+        out_ref[:, 1 - zh if far else zh] = result.astype(BF).reshape(4, 32, 224)
+    weight_send.wait_send()
+    for copy in pending + sends:
         copy.wait_send()
 
 
 CHUNKS = 4
 CHUNK = 4096 // CHUNKS
-EX_ORDERS = (("z", "y", "x"), ("x", "z", "y"), ("y", "x", "z"))
-EX_LANES = ((0, 256), (256, 640), (640, 1024))
+EX_ORDERS = (("x", "y"), ("y", "x"))
+EX_LANES = ((0, CHUNK // 2), (CHUNK // 2, CHUNK))
 SCALE = 192**-0.5 * 1.4426950408889634
 LAST = (((1,), (1,)), ((), ()))
 ROWS = 1024 // CHUNKS
@@ -416,20 +428,21 @@
         pltpu.VMEM((64, 8192), BF),
         pltpu.VMEM((32, 128, 512), BF),
         pltpu.VMEM((32, 512, 128), BF),
-        pltpu.VMEM((224, 4096), BF),
+        pltpu.VMEM((2, 224, 4096), BF),
         pltpu.VMEM((1024, 512), BF),
         pltpu.VMEM((2, ROWS, KEYS), f32),
         pltpu.VMEM((1024, 512), f32),
         pltpu.VMEM((1024, 128), f32),
         pltpu.VMEM((1024, 128), f32),
-        pltpu.VMEM((4, 4, 2, 32, 4096), BF),
-        pltpu.VMEM((4, 256, 224), f32),
-        pltpu.VMEM((6, 256, 224), BF),
-        sem((3,)),
-        sem((CHUNKS, 9, 3)),
-        sem((CHUNKS, 9, 3)),
-        sem((3,)),
-        sem((3,)),
+        pltpu.VMEM((4, 4, 32, 4096), BF),
+        pltpu.VMEM((2, 512, 224), f32),
+        pltpu.VMEM((8, 128, 224), BF),
+        pltpu.VMEM((8, 128, 224), BF),
+        sem((5,)),
+        sem((CHUNKS, 4, 3)),
+        sem((CHUNKS, 4, 3)),
+        sem((8,)),
+        sem((8,)),
     ]
     for slots, held in landing_shapes():
         scratch += [pltpu.VMEM(slots, BF), pltpu.VMEM(held, BF)]
@@ -438,7 +451,7 @@
     vmem = pl.BlockSpec(memory_space=pltpu.VMEM)
     return pl.pallas_call(
         layer_kernel,
-        out_shape=jax.ShapeDtypeStruct((256, 224), BF),
+        out_shape=jax.ShapeDtypeStruct((4, 2, 32, 224), BF),
         in_specs=[pl.BlockSpec(memory_space=pltpu.SMEM), vmem, vmem] + [hbm] * 9,
         out_specs=vmem,
         scratch_shapes=scratch,

time: 156 us -> 121 us (0.78); the launches traced: 153 us -> 121 us
  Pallas kernels: 147 us -> 115 us
    pallas_call x1, Pallas kernels: 147 us -> 115 us  [layer(): pl.pallas_call(layer_kernel, out_shape=jax.ShapeDtypeStruct((4, 2, 32, 22...]
where the time goes in v4:
time: 121 us
  Pallas kernels  115 us (95%)
  local copies, waits for them, and re-layouts  5.15 us (4%)
    pallas_call x1, Pallas kernels, layer(): pl.pallas_call(layer_kernel, out_shape=jax.ShapeDtypeStruct((4, 2, 32, 22...  115 us

profile of v4, /device:TPU:1, one launch (start us, length us, event | category | flops | bytes accessed | tf_op | source)
XLA Modules:
  0.0 120.9 jit_solution(5468364511391771529)
XLA Ops:
  0.7 1.4 %reshape.14.new_ref = bf16[32,576]{1,0:T(8,128)(2,1)} reshape(bf16[8,4,576]{2,1,0:T(4,128)(2,1)} %param.9) | data formatting | bytes 73728 | tf_op jit(solution)/shard_map/reshape | solution.py:469
  2.1 2.1 %copy.9 = bf16[32,32,192]{2,0,1:T(8,128)(2,1)} copy(bf16[32,32,192]{2,1,0:T(8,128)(2,1)} %bitcast.21) | data formatting | bytes 786432 | tf_op jit(solution)/shard_map/reshape | solution.py:467
  4.2 115.1 %layer.1 = bf16[4,2,32,224]{3,2,1,0:T(8,128)(2,1)} custom-call(s32[1]{0:T(128)S(6)} %copy.10.owner_ref, bf16[1024,192]{1,0:T(8,128)(2,1)} %bitcast.18, bf16[32,576]{1,0:T(8,128)(2,1)} %reshape.14.new_ref, bf16[32,128,512]{2,1,0:T(8,128)(2,1)} %key_hbm.1, bf16[32,512,128]{2,1,0:T(8,128)(2,1)} %value_hbm.1, bf16[224,4096]{1,0:T(8,128)(2,1)} %bitcast.19, ...), custom_call_target="tpu_custom_call" | custom-call | tf_op jit(solution)/shard_map/layer/pallas_call | solution.py:452
  119.3 1.6 %reshape.15 = bf16[64,4,224]{2,1,0:T(4,128)(2,1)} reshape(bf16[4,2,32,224]{3,2,1,0:T(8,128)(2,1)} %layer.1) | data formatting | bytes 229376 | tf_op jit(solution)/shard_map/reshape | solution.py:471

commit v5 on v4

v5 whole, which is shorter than its diff:
```python
import functools
import jax
import jax.numpy as jnp
from jax import lax
from jax.experimental import pallas as pl
from jax.experimental.pallas import tpu as pltpu
from jax.sharding import PartitionSpec as P

MESH = pl.DeviceIdType.MESH
BF = jnp.bfloat16


class Coord:
    def __init__(self):
        g, t = lax.axis_index("grp"), lax.axis_index("tp")
        self.x, self.y, self.z, self.c = g // 8, (g // 2) % 4, (g % 2) * 2 + t // 2, t % 2

    def at(self, **moved):
        x, y, z, c = (moved.get(k, getattr(self, k)) for k in "xyzc")
        return (x * 8 + y * 2 + z // 2, (z % 2) * 2 + c)


ORDERS = (("x", "y", "z"), ("y", "z", "x"), ("z", "x", "y"))
REGIONS = (
    (0, "A", 32, 0, 0),
    (0, "B", 16, 3, 0),
    (1, "A", 32, 1, 0),
    (1, "B", 16, 3, 2048),
    (2, "A", 32, 2, 0),
    (2, "R", 128, None, None),
)


def source_views(latent):
    return (
        latent.reshape(2, 8, 4, 2, 2, 32, 512),
        latent.reshape(2, 2, 8, 4, 2, 2, 16, 512),
        latent.reshape(2, 8, 2, 2, 4, 32, 512),
        latent.reshape(2, 2, 8, 2, 2, 4, 16, 512),
        latent.reshape(2, 2, 2, 2, 4, 4, 32, 512),
    )


def landing_shapes():
    shapes = []
    for lane, kind, unit, _, _ in REGIONS:
        dims = ((4, 4, 2), (4, 2, 4), (2, 4, 4))[lane]
        for step in range(3):
            if kind == "R":
                width = unit
                for d in dims[step + 1 :]:
                    width *= d
                shapes.append(((dims[step], 16, width), (16, width)))
            else:
                tail = dims[step + 1 :] + (unit, 128)
                shapes.append(((dims[step],) + tail, tail))
    return shapes


def layer_kernel(
    owner_ref, q_ref, new_ref, key_hbm, value_hbm, weight_hbm, v0, v1, v2, v3, v4, rope_ref, out_ref,
    lat_ref, rot_ref, key_ref, value_ref, weight_ref, qlat_ref, acc_ref, max_ref, sum_ref,
    att_ref, total_ref, part_ref, land_ref, weight_sem, ex_send, ex_recv, rs_send, rs_recv, *scratch
):
    me = Coord()
    views = (v0, v1, v2, v3, v4, rope_ref)
    landings = [(scratch[2 * i], scratch[2 * i + 1]) for i in range(36)]
    sc_send, sc_recv, sc_own, ag_send, ag_recv, sw_send, sw_recv = scratch[72:]
    key_copy = pltpu.make_async_copy(key_hbm, key_ref, weight_sem.at[0])
    value_copy = pltpu.make_async_copy(value_hbm, value_ref, weight_sem.at[1])
    zh, zl = me.z // 2, me.z % 2
    weight_copy = pltpu.make_async_copy(weight_hbm, weight_ref.at[zh], weight_sem.at[2])
    weight_sends = [
        pltpu.make_async_remote_copy(
            src_ref=weight_hbm.at[:, pl.ds(i * CHUNK, CHUNK)],
            dst_ref=weight_ref.at[zh, :, pl.ds(i * CHUNK, CHUNK)],
            send_sem=weight_sem.at[3 + i],
            recv_sem=weight_sem.at[3 + CHUNKS + i],
            device_id=me.at(z=(me.z + 2) % 4),
            device_id_type=MESH,
        )
        for i in range(CHUNKS)
    ]
    owner = owner_ref[0]
    owner_digit = {"x": owner // 8, "y": (owner // 2) % 4, "z": owner % 2}

    barrier = pltpu.get_barrier_semaphore()
    peers = [me.at(**{a: (getattr(me, a) + d) % 4}) for a in "xyz" for d in (1, 2, 3)]
    peers += [me.at(z=(me.z + d) % 4, c=1 - me.c) for d in range(4)]
    for peer in peers:
        pl.semaphore_signal(barrier, inc=1, device_id=peer, device_id_type=MESH)
    pl.semaphore_wait(barrier, len(peers))

    def own_digit(axis):
        return zh if axis == "z" else getattr(me, axis)

    rope_rows = pl.ds(pl.multiple_of(32 * me.c + 16 * zl, 16), 16)

    def source(h, region, digit):
        lane, kind, unit, tile, base = REGIONS[region]
        view = views[region]
        if kind == "R":
            return view.at[rope_rows, pl.ds(pl.multiple_of(4096 * h + 2048 * digit, 128), 2048)]
        cols = pl.ds(tile * 128, 128)
        if lane == 2:
            return view.at[h, me.c, digit, zl, :, :, :, cols]
        lead = (h, lane) if kind == "B" else (h,)
        if lane == 0:
            return view.at[lead + (me.c * 4 + digit, slice(None), slice(None), zl, slice(None), cols)]
        return view.at[lead + (me.c * 4 + digit, slice(None), zl, slice(None), slice(None), cols)]

    def part(h, region, step, digit):
        if step == 0:
            return source(h, region, digit)
        held = landings[h * 18 + region * 3 + step - 1][1]
        if REGIONS[region][1] == "R":
            width = landings[h * 18 + region * 3 + step][0].shape[2]
            return held.at[:, pl.ds(pl.multiple_of(digit * width, 128), width)]
        return held.at[digit]

    def scatter_copies(h, region, step):
        axis = ORDERS[REGIONS[region][0]][step]
        index = h * 18 + region * 3 + step
        slots = landings[index][0]
        mine = own_digit(axis)
        copies = []
        own = pltpu.make_async_copy(part(h, region, step, mine), slots.at[mine], sc_own.at[index])
        for d in (1, 2, 3) if axis != "z" else (2,):
            if axis == "z":
                target, digit = (me.z + 2) % 4, 1 - zh
            else:
                target = digit = (mine + d) % 4
            copies.append(
                pltpu.make_async_remote_copy(
                    src_ref=part(h, region, step, digit),
                    dst_ref=slots.at[mine],
                    send_sem=sc_send.at[index, d - 1],
                    recv_sem=sc_recv.at[index, d - 1],
                    device_id=me.at(**{axis: target}),
                    device_id_type=MESH,
                )
            )
        return own, copies

    def block(h, region, level, digits):
        lane, kind, unit, tile, base = REGIONS[region]
        count = unit * 4 ** (3 - level)
        place = 0
        for i in range(3):
            place = place * 4 + (digits[i] if i < level else 0)
        if kind == "R":
            place = place - digits[0] * 16 + (digits[0] // 2) * 16
            rows = pl.ds(pl.multiple_of(32 * me.c + 16 * (digits[0] % 2), 16), 16)
            return rot_ref.at[rows, pl.ds(pl.multiple_of(4096 * h + 128 * place, 128), count)]
        start = pl.multiple_of(4096 * h + base + unit * (64 * me.c + place), 16)
        return lat_ref.at[pl.ds(start, count), pl.ds(tile * 128, 128)]

    order = [ORDERS[r[0]] for r in REGIONS]
    digits = [tuple(getattr(me, a) for a in o) for o in order]
    pending = []

    def gather_start(h, region, level):
        axis = order[region][level - 1]
        ref = block(h, region, level, digits[region])
        copies = []
        for d in (1, 2, 3):
            copy = pltpu.make_async_remote_copy(
                src_ref=ref,
                dst_ref=ref,
                send_sem=ag_send.at[h * 6 + region, level - 1, d - 1],
                recv_sem=ag_recv.at[h * 6 + region, level - 1, d - 1],
                device_id=me.at(**{axis: (getattr(me, axis) + d) % 4}),
                device_id_type=MESH,
            )
            copy.start()
            copies.append(copy)
        return copies

    def prefix_half(h):
        started = []
        for region in range(6):
            own, copies = scatter_copies(h, region, 0)
            for copy in copies:
                copy.start()
            own.start()
            started.append((own, copies))
        for step in range(3):
            yield
            following = []
            for region in range(6):
                own, copies = started[region]
                own.wait()
                for copy in copies:
                    copy.wait_recv()
                pending.extend(copies)
                slots, held = landings[h * 18 + region * 3 + step]
                chosen = slots[owner_digit[order[region][step]]]
                if step < 2:
                    held[...] = chosen
                    own, copies = scatter_copies(h, region, step + 1)
                    for copy in copies:
                        copy.start()
                    own.start()
                    following.append((own, copies))
                else:
                    home = block(h, region, 3, digits[region])
                    home[...] = chosen
                    following.append(gather_start(h, region, 3))
            started = following
        swaps = []

        def swap(region, which, first):
            ref = block(h, region, 1, (first, 0, 0))
            copy = pltpu.make_async_remote_copy(
                src_ref=ref,
                dst_ref=ref,
                send_sem=sw_send.at[h * 6 + region, which],
                recv_sem=sw_recv.at[h * 6 + region, which],
                device_id=me.at(c=1 - me.c),
                device_id_type=MESH,
            )
            copy.start()
            swaps.append(copy)

        for level in (3, 2):
            yield
            following = []
            for region in range(6):
                for copy in started[region]:
                    copy.wait_recv()
                pending.extend(started[region])
                following.append(gather_start(h, region, level - 1))
            if level == 2:
                for region in range(6):
                    swap(region, 0, digits[region][0])
            started = following
        yield
        for d in (1, 3, 2):
            for region in range(6):
                started[region][d - 1].wait_recv()
                swap(region, d, (digits[region][0] + 4 - d) % 4)
        for region in range(6):
            pending.extend(started[region])
        yield
        for copy in swaps:
            copy.wait_recv()
        pending.extend(swaps)

    first, second = prefix_half(0), prefix_half(1)
    next(first)
    key_copy.start()
    value_copy.start()
    weight_copy.start()
    key_copy.wait()
    latent_queries(0, 8, q_ref, key_ref, qlat_ref)
    next(first)
    next(second)
    latent_queries(8, 16, q_ref, key_ref, qlat_ref)
    next(first)
    latent_queries(16, 24, q_ref, key_ref, qlat_ref)
    next(first)
    latent_queries(24, 32, q_ref, key_ref, qlat_ref)
    next(first)
    next(second)
    new_keys(q_ref, new_ref, qlat_ref, acc_ref, max_ref, sum_ref)
    next(first)
    next(second)
    next(second)
    next(second)
    next(first)
    next(second)
    for _ in first:
        pass
    all_rows(0, 2, q_ref, qlat_ref, lat_ref, rot_ref, acc_ref, max_ref, sum_ref)
    weight_sends[0].start()
    all_rows(2, 3, q_ref, qlat_ref, lat_ref, rot_ref, acc_ref, max_ref, sum_ref)
    next(second)
    all_rows(3, 4, q_ref, qlat_ref, lat_ref, rot_ref, acc_ref, max_ref, sum_ref)
    for copy in weight_sends[1:]:
        copy.start()
    for _ in second:
        pass

    def exchange(chunk):
        for step in range(2):
            copies = []
            for lane, (low, high) in enumerate(EX_LANES):
                axis = EX_ORDERS[lane][step]
                done = EX_ORDERS[lane][:step]
                cols = pl.ds(chunk * CHUNK + low, high - low)
                where = tuple(slice(None) if a in done else getattr(me, a) for a in "xy")
                ref = att_ref.at[where + (slice(None), cols)]
                for d in (1, 2, 3):
                    copy = pltpu.make_async_remote_copy(
                        src_ref=ref,
                        dst_ref=ref,
                        send_sem=ex_send.at[chunk, lane * 2 + step, d - 1],
                        recv_sem=ex_recv.at[chunk, lane * 2 + step, d - 1],
                        device_id=me.at(**{axis: (getattr(me, axis) + d) % 4}),
                        device_id_type=MESH,
                    )
                    copy.start()
                    copies.append(copy)
            yield
            for copy in copies:
                copy.wait_recv()
            pending.extend(copies)

    def partial_out(chunk, half):
        cols = pl.ds(chunk * CHUNK, CHUNK)
        values = att_ref[:, :, :, cols].reshape(512, CHUNK)
        return dot_last(values, weight_ref[half, :, cols])

    active = []
    for chunk in range(CHUNKS):
        chunk_rows(chunk * ROWS, 4, 8, q_ref, qlat_ref, lat_ref, rot_ref, acc_ref, max_ref, sum_ref)
        if active:
            next(active[-1])
        if chunk == 0:
            value_copy.wait()
        attended_values(chunk, acc_ref, sum_ref, value_ref, att_ref, (me.x, me.y))
        active.append(exchange(chunk))
        next(active[-1])
    weight_copy.wait()
    for chunk in range(CHUNKS - 1):
        for _ in active[chunk]:
            pass
        if chunk == 0:
            next(active[-1])

        weight_sends[chunk].wait_recv()

        @pl.loop(0, 2)
        def _(half):
            term = partial_out(chunk, half)
            total_ref[half] = term if chunk == 0 else total_ref[half] + term
    for _ in active[-1]:
        pass
    weight_sends[-1].wait_recv()
    sends = []
    for far in (1, 0):
        half = 1 - zh if far else zh
        total_ref[half] = total_ref[half] + partial_out(CHUNKS - 1, half)
        for flip_z in (1, 0):
            for flip_c in (1, 0):
                target_l = 1 - zl if flip_z else zl
                target_c = 1 - me.c if flip_c else me.c
                slot = 4 * far + 2 * flip_z + flip_c
                if slot == 0:
                    continue
                rows = pl.ds(pl.multiple_of((target_l * 2 + target_c) * 128, 128), 128)
                part_ref[slot] = total_ref[half, rows, :].astype(BF)
                copy = pltpu.make_async_remote_copy(
                    src_ref=part_ref.at[slot],
                    dst_ref=land_ref.at[slot],
                    send_sem=rs_send.at[slot],
                    recv_sem=rs_recv.at[slot],
                    device_id=me.at(z=half * 2 + target_l, c=target_c),
                    device_id_type=MESH,
                )
                copy.start()
                sends.append(copy)
    for copy in sends:
        copy.wait_recv()
    own_rows = pl.ds(pl.multiple_of((zl * 2 + me.c) * 128, 128), 128)
    for far in (0, 1):
        result = land_ref[4 * far + 1].astype(jnp.float32) + land_ref[4 * far + 2].astype(jnp.float32)
        result = result + land_ref[4 * far + 3].astype(jnp.float32)
        result = result + (land_ref[4].astype(jnp.float32) if far else total_ref[zh, own_rows, :])
        out_ref[:, 1 - zh if far else zh] = result.astype(BF).reshape(4, 32, 224)
    for copy in pending + sends + weight_sends:
        copy.wait_send()


CHUNKS = 4
CHUNK = 4096 // CHUNKS
EX_ORDERS = (("x", "y"), ("y", "x"))
EX_LANES = ((0, CHUNK // 2), (CHUNK // 2, CHUNK))
SCALE = 192**-0.5 * 1.4426950408889634
LAST = (((1,), (1,)), ((), ()))
ROWS = 1024 // CHUNKS
KEYS = 1024


def dot(a, b):
    return jnp.dot(a, b, preferred_element_type=jnp.float32)


def dot_last(a, b):
    return lax.dot_general(a, b, LAST, preferred_element_type=jnp.float32)


def latent_queries(low, high, q_ref, key_ref, qlat_ref):
    @pl.loop(low, high, unroll=4)
    def _(h):
        rows = pl.ds(pl.multiple_of(h * 32, 32), 32)
        qlat_ref[rows, :] = dot(q_ref[rows, 0:128], key_ref[h]).astype(BF)


def new_keys(q_ref, new_ref, qlat_ref, acc_ref, max_ref, sum_ref):
    @pl.loop(0, 4)
    def _(r):
        rows = pl.ds(pl.multiple_of(r * ROWS, ROWS), ROWS)
        scores = dot_last(qlat_ref[rows, :], new_ref[:, 0:512])
        scores = (scores + dot_last(q_ref[rows, 128:192], new_ref[:, 512:576])) * SCALE
        row = lax.broadcasted_iota(jnp.int32, (ROWS, 32), 0) % 32
        key = lax.broadcasted_iota(jnp.int32, (ROWS, 32), 1)
        visible = (row // 4 == key // 4) & (key <= row)
        top = jnp.max(jnp.where(visible, scores, -jnp.inf), axis=1, keepdims=True)
        e = jnp.where(visible, jnp.exp2(jnp.where(visible, scores, top) - top), 0.0)
        max_ref[rows, :] = jnp.broadcast_to(top, (ROWS, 128))
        sum_ref[rows, :] = jnp.broadcast_to(jnp.sum(e, axis=1, keepdims=True), (ROWS, 128))
        acc_ref[rows, :] = dot(e.astype(BF), new_ref[:, 0:512])


def block_scores(rows, k, q_ref, qlat_ref, lat_ref, rot_ref):
    keys = pl.ds(pl.multiple_of(k * KEYS, KEYS), KEYS)
    return dot_last(qlat_ref[rows, :], lat_ref[keys, :]) + dot(q_ref[rows, 128:192], rot_ref[:, keys])


def take(rows, k, s, lat_ref, acc_ref, max_ref, sum_ref):
    keys = pl.ds(pl.multiple_of(k * KEYS, KEYS), KEYS)
    old = max_ref[rows, :]
    new = jnp.maximum(old, jnp.max(s, axis=1, keepdims=True) * SCALE)
    max_ref[rows, :] = new
    shrink = jnp.exp2(old - new)
    e = jnp.exp2(s * SCALE - new[:, 0:1])
    sum_ref[rows, :] = sum_ref[rows, :] * shrink + jnp.sum(e, axis=1, keepdims=True)
    acc_ref[rows, :] = acc_ref[rows, :] * shrink[:, 0:1] + dot(e.astype(BF), lat_ref[keys, :])


def all_rows(low, high, q_ref, qlat_ref, lat_ref, rot_ref, acc_ref, max_ref, sum_ref):
    @pl.loop(low, high)
    def _(k):
        halves = [pl.ds(0, 512), pl.ds(512, 512)]
        scores = [block_scores(rows, k, q_ref, qlat_ref, lat_ref, rot_ref) for rows in halves]
        for rows, s in zip(halves, scores):
            take(rows, k, s, lat_ref, acc_ref, max_ref, sum_ref)


def chunk_rows(row, low, high, q_ref, qlat_ref, lat_ref, rot_ref, acc_ref, max_ref, sum_ref):
    rows = pl.ds(row, ROWS)
    s = block_scores(rows, low, q_ref, qlat_ref, lat_ref, rot_ref)
    for k in range(low, high):
        following = block_scores(rows, k + 1, q_ref, qlat_ref, lat_ref, rot_ref) if k + 1 < high else None
        take(rows, k, s, lat_ref, acc_ref, max_ref, sum_ref)
        s = following


def attended_values(chunk, acc_ref, sum_ref, value_ref, att_ref, place):
    heads = 32 // CHUNKS

    @pl.loop(chunk * heads, (chunk + 1) * heads, unroll=4)
    def _(h):
        rows = pl.ds(pl.multiple_of(h * 32, 32), 32)
        context = (acc_ref[rows, :] / sum_ref[rows, 0:1]).astype(BF)
        cols = pl.ds(pl.multiple_of(h * 128, 128), 128)
        att_ref[place + (slice(None), cols)] = dot(context, value_ref[h]).astype(BF)


def layer(owner_index, queries, new_kv, key_up, value_up, out_weight, latent, rope):
    sem = pltpu.SemaphoreType.DMA
    f32 = jnp.float32
    scratch = [
        pltpu.VMEM((8192, 512), BF),
        pltpu.VMEM((64, 8192), BF),
        pltpu.VMEM((32, 128, 512), BF),
        pltpu.VMEM((32, 512, 128), BF),
        pltpu.VMEM((2, 224, 4096), BF),
        pltpu.VMEM((1024, 512), BF),
        pltpu.VMEM((1024, 512), f32),
        pltpu.VMEM((1024, 128), f32),
        pltpu.VMEM((1024, 128), f32),
        pltpu.VMEM((4, 4, 32, 4096), BF),
        pltpu.VMEM((2, 512, 224), f32),
        pltpu.VMEM((8, 128, 224), BF),
        pltpu.VMEM((8, 128, 224), BF),
        sem((3 + 2 * CHUNKS,)),
        sem((CHUNKS, 4, 3)),
        sem((CHUNKS, 4, 3)),
        sem((8,)),
        sem((8,)),
    ]
    for slots, held in landing_shapes() * 2:
        scratch += [pltpu.VMEM(slots, BF), pltpu.VMEM(held, BF)]
    scratch += [sem((36, 3)), sem((36, 3)), sem((36,)), sem((12, 3, 3)), sem((12, 3, 3)), sem((12, 4)), sem((12, 4))]
    hbm = pl.BlockSpec(memory_space=pl.ANY)
    vmem = pl.BlockSpec(memory_space=pltpu.VMEM)
    return pl.pallas_call(
        layer_kernel,
        out_shape=jax.ShapeDtypeStruct((4, 2, 32, 224), BF),
        in_specs=[pl.BlockSpec(memory_space=pltpu.SMEM), vmem, vmem] + [hbm] * 9,
        out_specs=vmem,
        scratch_shapes=scratch,
        compiler_params=pltpu.CompilerParams(
            collective_id=0, has_side_effects=True, vmem_limit_bytes=60 << 20
        ),
        name="layer",
    )(owner_index, queries, new_kv, key_up, value_up, out_weight, *source_views(latent), rope)


def body(queries, new_kv, owner_index, prefix_latent, prefix_rope, key_up, value_up, out_weight):
    samples, steps, heads, width = queries.shape
    rows = jnp.transpose(queries.reshape(samples * steps, heads, width), (1, 0, 2)).reshape(-1, width)
    out = layer(
        owner_index, rows, new_kv.reshape(samples * steps, -1), key_up, value_up, out_weight.T, prefix_latent[0], prefix_rope[0]
    )
    return out.reshape(64, steps, -1)


def solution(mesh):
    return jax.shard_map(
        body,
        mesh=mesh,
        in_specs=(
            P("grp", None, "tp", None),
            P("grp", None, None),
            P(),
            P("grp", None, None),
            P("grp", None, None),
            P("tp", None, None),
            P("tp", None, None),
            P("tp", "grp"),
        ),
        out_specs=P("tp", None, "grp"),
        check_vma=False,
    )
```

time: 121 us -> 163 us (1.35)
  Pallas kernels: 115 us -> 156 us
    pallas_call x1, Pallas kernels: 115 us -> 156 us  [layer(): pl.pallas_call(layer_kernel, out_shape=jax.ShapeDtypeStruct((4, 2, 32, 22...]
where the time goes in v5:
time: 163 us; the launch traced here: 161 us
  Pallas kernels  156 us (96%)
  local copies, waits for them, and re-layouts  5.15 us (3%)
    pallas_call x1, Pallas kernels, layer(): pl.pallas_call(layer_kernel, out_shape=jax.ShapeDtypeStruct((4, 2, 32, 22...  156 us

profile of v5, /device:TPU:1, one launch (start us, length us, event | category | flops | bytes accessed | tf_op | source)
XLA Modules:
  0.0 161.4 jit_solution(11219486009841365922)
XLA Ops:
  0.7 1.4 reshape.14.new_ref
  2.1 2.1 %copy.9 = bf16[32,32,192]{2,0,1:T(8,128)(2,1)} copy(bf16[32,32,192]{2,1,0:T(8,128)(2,1)} %bitcast.21) | data formatting | bytes 786432 | tf_op jit(solution)/shard_map/reshape | solution.py:504
  4.2 155.6 %layer.1 = bf16[4,2,32,224]{3,2,1,0:T(8,128)(2,1)} custom-call(s32[1]{0:T(128)S(6)} %copy.10.owner_ref, bf16[1024,192]{1,0:T(8,128)(2,1)} %bitcast.18, bf16[32,576]{1,0:T(8,128)(2,1)} %reshape.14.new_ref, bf16[32,128,512]{2,1,0:T(8,128)(2,1)} %key_hbm.1, bf16[32,512,128]{2,1,0:T(8,128)(2,1)} %value_hbm.1, bf16[224,4096]{1,0:T(8,128)(2,1)} %bitcast.19, ...), custom_call_target="tpu_custom_call" | custom-call | tf_op jit(solution)/shard_map/layer/pallas_call | solution.py:489
  159.8 1.6 reshape.15

commit v6 on v0

v6 whole, which is shorter than its diff:
```python
import functools
import jax
import jax.numpy as jnp
from jax import lax
from jax.experimental import pallas as pl
from jax.experimental.pallas import tpu as pltpu
from jax.sharding import PartitionSpec as P

MESH = pl.DeviceIdType.MESH
BF = jnp.bfloat16
F32 = jnp.float32
CHUNKS = 4
CHUNK = 4096 // CHUNKS
ROWS = 1024 // CHUNKS


class Coord:
    def __init__(self):
        g, t = lax.axis_index("grp"), lax.axis_index("tp")
        self.x, self.y, self.z, self.c = g // 8, (g // 2) % 4, (g % 2) * 2 + t // 2, t % 2

    def at(self, **moved):
        x, y, z, c = (moved.get(k, getattr(self, k)) for k in "xyzc")
        return (x * 8 + y * 2 + z // 2, (z % 2) * 2 + c)


ORDERS = (("x", "y", "z"), ("y", "z", "x"), ("z", "x", "y"), ("z", "x", "y"))
BASES = (0, 3072, 6144)
SHARE = ((768, 192, 96), (768, 384, 96), (512, 128, 32), (2048, 512, 128))
ROPE = 3


def landing_shapes():
    shapes = []
    for region in range(4):
        for step in range(3):
            share = SHARE[region][step]
            one = (32, share) if region == ROPE else (share, 256 if region == 2 else 128)
            slots = 2 if ORDERS[region][step] == "z" else 4
            shapes.append(((slots,) + one, one))
    return shapes


def wait_bytes(ref, sem):
    pltpu.make_async_copy(ref, ref, sem).wait()


def layer_kernel(
    owner_ref, q_ref, new_ref, key_hbm, value_hbm, weight_hbm, latent_hbm, rope_hbm, out_ref,
    lat_ref, rot_ref, key_ref, value_ref, weight_ref, qlat_ref, acc_ref, max_ref, sum_ref,
    att_ref, total_ref, part_ref, land_ref, local_sem, weight_send, weight_recv, sc_send, sc_recv, sc_own,
    ag_send, ag_recv, last_send, last_recv, sw_send, sw_recv, ex_send, ex_recv, rs_sem, *landings
):
    me = Coord()
    zh, zl = me.z // 2, me.z % 2
    owner = owner_ref[0]
    owner_digit = {"x": owner // 8, "y": (owner // 2) % 4, "z": owner % 2}
    key_copy = pltpu.make_async_copy(key_hbm, key_ref, local_sem.at[0])
    value_copy = pltpu.make_async_copy(value_hbm, value_ref, local_sem.at[1])
    weight_copy = pltpu.make_async_copy(weight_hbm, weight_ref.at[zh], local_sem.at[2])
    drains = []

    def send(src, dst, send_sem, recv_sem, device):
        copy = pltpu.make_async_remote_copy(
            src_ref=src, dst_ref=dst, send_sem=send_sem, recv_sem=recv_sem, device_id=device, device_id_type=MESH
        )
        copy.start()
        return copy

    def beside(axis, d):
        return me.at(**{axis: (getattr(me, axis) + d) % 4})

    barrier = pltpu.get_barrier_semaphore()
    peers = [beside(a, d) for a in "xyz" for d in (1, 2, 3)]
    peers += [me.at(z=(me.z + d) % 4, c=1 - me.c) for d in range(4)]
    peers += [me.at(x=(me.x + i) % 4, y=(me.y + j) % 4) for i in (1, 2, 3) for j in (1, 2, 3)]
    for peer in peers:
        pl.semaphore_signal(barrier, inc=1, device_id=peer, device_id_type=MESH)
    pl.semaphore_wait(barrier, len(peers))

    cols = pl.ds(pl.multiple_of(256 * me.c, 256), 256)
    rope_rows = pl.ds(pl.multiple_of(32 * me.c, 32), 32)

    def own_digit(axis):
        return zh if axis == "z" else getattr(me, axis)

    tile = pl.ds(pl.multiple_of(256 * me.c + 128 * zl, 128), 128)

    def source(region, digit):
        if region == ROPE:
            return rope_hbm.at[rope_rows, pl.ds(pl.multiple_of(4096 * digit + 2048 * zl, 128), 2048)]
        if region == 2:
            return latent_hbm.at[pl.ds(pl.multiple_of(6144 + 1024 * digit + 512 * zl, 512), 512), cols]
        return latent_hbm.at[pl.ds(pl.multiple_of(BASES[region] + 768 * digit, 256), 768), tile]

    def part(region, step, digit):
        if step == 0:
            return source(region, digit)
        held = landings[2 * (region * 3 + step - 1) + 1]
        share = SHARE[region][step]
        if region == ROPE:
            return held.at[:, pl.ds(pl.multiple_of(digit * share, 128), share)]
        return held.at[pl.ds(pl.multiple_of(digit * share, 32), share)]

    def scatter(region, step):
        axis = ORDERS[region][step]
        index = region * 3 + step
        slots = landings[2 * index]
        mine = own_digit(axis)
        if axis == "z":
            send(part(region, step, 1 - zh), slots.at[mine], sc_send.at[index], sc_recv.at[index], beside("z", 2))
        else:
            for d in (1, 3, 2):
                digit = (mine + d) % 4
                send(part(region, step, digit), slots.at[mine], sc_send.at[index], sc_recv.at[index], beside(axis, d))
        pltpu.make_async_copy(part(region, step, mine), slots.at[mine], sc_own.at[index]).start()
        others = slots.at[pl.ds(0, slots.shape[0] - 1)]
        drains.append((others, sc_send.at[index]))

    def pick(region, step):
        index = region * 3 + step
        slots = landings[2 * index]
        wait_bytes(slots.at[0], sc_own.at[index])
        wait_bytes(slots.at[pl.ds(0, slots.shape[0] - 1)], sc_recv.at[index])
        return slots[owner_digit[ORDERS[region][step]]]

    def extent(region, level):
        if region in (0, 1):
            return (768, (192, 384)[region], 96)[level - 1], level == 3 or (region, level) == (1, 2)
        return (32, 128)[region - 2] * 4 ** (3 - level), False

    def block(region, level, digits):
        count, narrow = extent(region, level)
        if region == ROPE or region == 2:
            place = digits[0] * 16
            for i in range(1, level):
                place = place + digits[i] * 4 ** (2 - i)
            if region == ROPE:
                return rot_ref.at[rope_rows, pl.ds(pl.multiple_of(128 * place, 128), count)]
            return lat_ref.at[pl.ds(pl.multiple_of(6144 + 32 * place, 32), count), cols]
        start = BASES[region] + digits[0] * 768
        if region == 0:
            start = start + (digits[1] * 192 if level > 1 else 0) + (zh * 96 if level > 2 else 0)
        else:
            start = start + (zh * 384 if level > 1 else 0) + (digits[2] * 96 if level > 2 else 0)
        return lat_ref.at[pl.ds(pl.multiple_of(start, 32), count), tile if narrow else cols]

    digits = [tuple(getattr(me, a) for a in o) for o in ORDERS]

    def three(region, level):
        count, narrow = extent(region, level)
        if region == ROPE:
            return rot_ref.at[0:32, 0 : 3 * count]
        return lat_ref.at[0 : 3 * count, 0 : 128 if narrow else 256]

    def gather(region, level):
        ref = block(region, level, digits[region])
        sems = ag_send.at[region * 3 + level - 1], ag_recv.at[region * 3 + level - 1]
        for d in (1, 3, 2):
            send(ref, ref, *sems, beside(ORDERS[region][level - 1], d))
        drains.append((three(region, level), sems[0]))

    def gathered(region, level):
        wait_bytes(three(region, level), ag_recv.at[region * 3 + level - 1])

    def rope_plane():
        ref = block(ROPE, 3, digits[ROPE])
        sems = ag_send.at[ROPE * 3 + 2], ag_recv.at[ROPE * 3 + 2]
        for i in range(4):
            for j in range(4):
                if i or j:
                    send(ref, ref, *sems, me.at(x=(me.x + i) % 4, y=(me.y + j) % 4))
        drains.append((rot_ref.at[0:32, 0:1920], sems[0]))

    def swap(d):
        for region in range(3):
            ref = block(region, 1, ((digits[region][0] + 4 - d) % 4, 0, 0))
            send(ref, ref, sw_send.at[d], sw_recv.at[d], me.at(c=1 - me.c))
        drains.append((lat_ref.at[0:2048, 0:256], sw_send.at[d]))

    def swapped(d):
        wait_bytes(lat_ref.at[0:2048, 0:256], sw_recv.at[d])

    def send_weight(i):
        where = pl.ds(i * CHUNK, CHUNK)
        ref = weight_ref.at[zh, :, where]
        send(weight_hbm.at[:, where], ref, weight_send.at[i], weight_recv.at[i], beside("z", 2))
        drains.append((ref, weight_send.at[i]))

    for region in range(4):
        scatter(region, 0)
    key_copy.start()
    value_copy.start()
    weight_copy.start()
    key_copy.wait()
    latent_queries(0, 16, q_ref, key_ref, qlat_ref)
    for step in range(2):
        for region in (ROPE, 0, 1, 2):
            chosen = pick(region, step)
            landings[2 * (region * 3 + step) + 1][...] = chosen
            scatter(region, step + 1)
        if step == 0:
            send_weight(0)
            latent_queries(16, 32, q_ref, key_ref, qlat_ref)
    for region in (ROPE, 0, 1, 2):
        home = block(region, 3, digits[region])
        home[...] = pick(region, 2)
        if region == ROPE:
            rope_plane()
        else:
            gather(region, 3)
    send_weight(1)
    new_keys(q_ref, new_ref, qlat_ref, acc_ref, max_ref, sum_ref)
    wait_bytes(rot_ref.at[0:32, 0:1920], ag_recv.at[ROPE * 3 + 2])
    gather(ROPE, 1)
    for region in range(3):
        gathered(region, 3)
        gather(region, 2)
    gathered(ROPE, 1)
    send(rot_ref.at[rope_rows], rot_ref.at[rope_rows], sw_send.at[4], sw_recv.at[4], me.at(c=1 - me.c))
    drains.append((rot_ref.at[0:32], sw_send.at[4]))
    for region in range(3):
        gathered(region, 2)
        ref = block(region, 1, digits[region])
        for d in (1, 3, 2):
            send(ref, ref, last_send.at[d - 1], last_recv.at[d - 1], beside(ORDERS[region][0], d))
    for d in (1, 2, 3):
        drains.append((lat_ref.at[0:2048, 0:256], last_send.at[d - 1]))
    swap(0)

    def arrived(d):
        wait_bytes(lat_ref.at[0:2048, 0:256], last_recv.at[d - 1])

    def quarter(d):
        sizes = (768, 768, 512)
        starts = [BASES[r] + sizes[r] * ((digits[r][0] + 4 - d) % 4) for r in range(3)]
        return [pl.ds(pl.multiple_of(s, 256), n) for s, n in zip(starts, sizes)]

    attend = functools.partial(
        attend_rows, q_ref, qlat_ref, lat_ref, rot_ref, acc_ref, max_ref, sum_ref
    )
    def rows_of(i):
        return pl.ds(pl.multiple_of(i * 256, 256), 256)

    wait_bytes(rot_ref.at[0:32], sw_recv.at[4])
    swapped(0)

    @pl.loop(0, 2)
    def _(i):
        attend([(rows_of(2 * i), quarter(0)), (rows_of(2 * i + 1), quarter(0))])

    arrived(1)
    swap(1)
    send_weight(2)
    send_weight(3)
    swapped(1)
    for i in (0, 1):
        attend([(rows_of(2 * i), quarter(1)), (rows_of(2 * i + 1), quarter(1))])
        arrived((3, 2)[i])
        swap((3, 2)[i])
    swapped(3)
    swapped(2)

    def exchange(chunk):
        cols = [pl.ds(chunk * CHUNK + lane * (CHUNK // 2), CHUNK // 2) for lane in (0, 1)]
        whole = pl.ds(chunk * CHUNK, CHUNK)
        sems = [(ex_send.at[chunk * 3 + i], ex_recv.at[chunk * 3 + i]) for i in range(3)]
        for lane, axis in enumerate("xy"):
            ref = att_ref.at[me.x, me.y, :, cols[lane]]
            for d in (1, 3, 2):
                send(ref, ref, *sems[0], beside(axis, d))
        total = att_ref.at[0, 0:3, :, whole]
        drains.append((total, sems[0][0]))
        yield
        wait_bytes(total, sems[0][1])
        lines = [lambda y, s=slice(None): att_ref.at[s, y, :, cols[0]], lambda x, s=slice(None): att_ref.at[x, s, :, cols[1]]]
        for lane, axis in enumerate("yx"):
            ref = lines[lane](getattr(me, axis))
            for d in (1, 3):
                send(ref, ref, *sems[1], beside(axis, d))
        total = att_ref.at[0:2, :, :, whole]
        drains.append((total, sems[1][0]))
        yield
        wait_bytes(total, sems[1][1])
        for lane, axis in enumerate("yx"):
            for d, share in ((1, pl.ds(0, 2)), (3, pl.ds(2, 2))):
                ref = lines[lane]((getattr(me, axis) + 4 - d) % 4, share)
                send(ref, ref, *sems[2], beside(axis, d))
        total = att_ref.at[0:1, :, :, whole]
        drains.append((total, sems[2][0]))
        yield
        wait_bytes(total, sems[2][1])

    def partial_out(chunk, half):
        where = pl.ds(chunk * CHUNK, CHUNK)
        return dot_last(att_ref[:, :, :, where].reshape(512, CHUNK), weight_ref[half, :, where])

    active = []
    for chunk in range(CHUNKS):
        rows = pl.ds(chunk * ROWS, ROWS)
        attend([(rows, quarter(3)), (rows, quarter(2))])
        for other in active[-2:]:
            next(other)
        if chunk == 0:
            value_copy.wait()
        attended_values(chunk, acc_ref, sum_ref, value_ref, att_ref, (me.x, me.y))
        active.append(exchange(chunk))
        next(active[-1])
    weight_copy.wait()
    next(active[2])
    next(active[3])
    for chunk in range(CHUNKS - 1):
        for _ in active[chunk]:
            pass
        wait_bytes(weight_ref.at[zh, :, pl.ds(chunk * CHUNK, CHUNK)], weight_recv.at[chunk])

        @pl.loop(0, 2)
        def _(half):
            term = partial_out(chunk, half)
            total_ref[half] = term if chunk == 0 else total_ref[half] + term

        if chunk == 1:
            next(active[3])
    for _ in active[-1]:
        pass
    wait_bytes(weight_ref.at[zh, :, pl.ds(3 * CHUNK, CHUNK)], weight_recv.at[3])
    for far in (1, 0):
        half = 1 - zh if far else zh
        total_ref[half] = total_ref[half] + partial_out(CHUNKS - 1, half)
        for flip_z in (1, 0):
            for flip_c in (1, 0):
                target_l = 1 - zl if flip_z else zl
                target_c = 1 - me.c if flip_c else me.c
                slot = 4 * far + 2 * flip_z + flip_c
                if slot == 0:
                    continue
                rows = pl.ds(pl.multiple_of((target_l * 2 + target_c) * 128, 128), 128)
                part_ref[slot] = total_ref[half, rows, :].astype(BF)
                send(
                    part_ref.at[slot], land_ref.at[slot], rs_sem.at[0], rs_sem.at[1],
                    me.at(z=half * 2 + target_l, c=target_c),
                )
    wait_bytes(land_ref.at[1:8], rs_sem.at[1])
    drains.append((land_ref.at[1:8], rs_sem.at[0]))
    own_rows = pl.ds(pl.multiple_of((zl * 2 + me.c) * 128, 128), 128)
    for far in (0, 1):
        result = land_ref[4 * far + 1].astype(F32) + land_ref[4 * far + 2].astype(F32)
        result = result + land_ref[4 * far + 3].astype(F32)
        result = result + (land_ref[4].astype(F32) if far else total_ref[zh, own_rows, :])
        out_ref[:, 1 - zh if far else zh] = result.astype(BF).reshape(4, 32, 224)
    for ref, sem in drains:
        wait_bytes(ref, sem)


SCALE = 192**-0.5 * 1.4426950408889634
LAST = (((1,), (1,)), ((), ()))


def dot(a, b):
    return jnp.dot(a, b, preferred_element_type=jnp.float32)


def dot_last(a, b):
    return lax.dot_general(a, b, LAST, preferred_element_type=jnp.float32)


def latent_queries(low, high, q_ref, key_ref, qlat_ref):
    @pl.loop(low, high, unroll=4)
    def _(h):
        rows = pl.ds(pl.multiple_of(h * 32, 32), 32)
        qlat_ref[rows, :] = dot(q_ref[rows, 0:128], key_ref[h]).astype(BF)


def new_keys(q_ref, new_ref, qlat_ref, acc_ref, max_ref, sum_ref):
    @pl.loop(0, CHUNKS)
    def _(r):
        rows = pl.ds(pl.multiple_of(r * ROWS, ROWS), ROWS)
        scores = dot_last(qlat_ref[rows, :], new_ref[:, 0:512])
        scores = (scores + dot_last(q_ref[rows, 128:192], new_ref[:, 512:576])) * SCALE
        row = lax.broadcasted_iota(jnp.int32, (ROWS, 32), 0) % 32
        key = lax.broadcasted_iota(jnp.int32, (ROWS, 32), 1)
        visible = (row // 4 == key // 4) & (key <= row)
        top = jnp.max(jnp.where(visible, scores, -jnp.inf), axis=1, keepdims=True)
        e = jnp.where(visible, jnp.exp2(jnp.where(visible, scores, top) - top), 0.0)
        max_ref[rows, :] = jnp.broadcast_to(top, (ROWS, 128))
        sum_ref[rows, :] = jnp.broadcast_to(jnp.sum(e, axis=1, keepdims=True), (ROWS, 128))
        acc_ref[rows, :] = dot(e.astype(BF), new_ref[:, 0:512])


def attend_rows(q_ref, qlat_ref, lat_ref, rot_ref, acc_ref, max_ref, sum_ref, items):
    scores = [
        [dot_last(qlat_ref[rows, :], lat_ref[keys, :]) + dot(q_ref[rows, 128:192], rot_ref[:, keys]) for keys in key_slices]
        for rows, key_slices in items
    ]
    for (rows, key_slices), parts in zip(items, scores):
        old = max_ref[rows, :]
        top = functools.reduce(jnp.maximum, [jnp.max(s, axis=1, keepdims=True) for s in parts])
        new = jnp.maximum(old, top * SCALE)
        max_ref[rows, :] = new
        shrink = jnp.exp2(old - new)
        total = sum_ref[rows, :] * shrink
        acc = acc_ref[rows, :] * shrink[:, 0:1]
        for s, keys in zip(parts, key_slices):
            e = jnp.exp2(s * SCALE - new[:, 0:1])
            total = total + jnp.sum(e, axis=1, keepdims=True)
            acc = acc + dot(e.astype(BF), lat_ref[keys, :])
        sum_ref[rows, :] = total
        acc_ref[rows, :] = acc


def attended_values(chunk, acc_ref, sum_ref, value_ref, att_ref, place):
    heads = 32 // CHUNKS

    @pl.loop(chunk * heads, (chunk + 1) * heads, unroll=4)
    def _(h):
        rows = pl.ds(pl.multiple_of(h * 32, 32), 32)
        context = (acc_ref[rows, :] / sum_ref[rows, 0:1]).astype(BF)
        cols = pl.ds(pl.multiple_of(h * 128, 128), 128)
        att_ref[place + (slice(None), cols)] = dot(context, value_ref[h]).astype(BF)


def layer(owner_index, queries, new_kv, key_up, value_up, out_weight, latent, rope):
    sem = pltpu.SemaphoreType.DMA
    vm = pltpu.VMEM
    scratch = [
        vm((8192, 512), BF),
        vm((64, 8192), BF),
        vm((32, 128, 512), BF),
        vm((32, 512, 128), BF),
        vm((2, 224, 4096), BF),
        vm((1024, 512), BF),
        vm((1024, 512), F32),
        vm((1024, 128), F32),
        vm((1024, 128), F32),
        vm((4, 4, 32, 4096), BF),
        vm((2, 512, 224), F32),
        vm((8, 128, 224), BF),
        vm((8, 128, 224), BF),
        sem((3,)),
        sem((CHUNKS,)),
        sem((CHUNKS,)),
        sem((12,)),
        sem((12,)),
        sem((12,)),
        sem((12,)),
        sem((12,)),
        sem((3,)),
        sem((3,)),
        sem((5,)),
        sem((5,)),
        sem((3 * CHUNKS,)),
        sem((3 * CHUNKS,)),
        sem((2,)),
    ]
    for slots, held in landing_shapes():
        scratch += [vm(slots, BF), vm(held, BF)]
    hbm = pl.BlockSpec(memory_space=pl.ANY)
    vmem = pl.BlockSpec(memory_space=pltpu.VMEM)
    return pl.pallas_call(
        layer_kernel,
        out_shape=jax.ShapeDtypeStruct((4, 2, 32, 224), BF),
        in_specs=[pl.BlockSpec(memory_space=pltpu.SMEM), vmem, vmem] + [hbm] * 5,
        out_specs=vmem,
        scratch_shapes=scratch,
        compiler_params=pltpu.CompilerParams(
            collective_id=0, has_side_effects=True, vmem_limit_bytes=60 << 20
        ),
        name="layer",
    )(owner_index, queries, new_kv, key_up, value_up, out_weight, latent, rope)


def body(queries, new_kv, owner_index, prefix_latent, prefix_rope, key_up, value_up, out_weight):
    samples, steps, heads, width = queries.shape
    rows = jnp.transpose(queries.reshape(samples * steps, heads, width), (1, 0, 2)).reshape(-1, width)
    out = layer(
        owner_index, rows, new_kv.reshape(samples * steps, -1), key_up, value_up, out_weight.T, prefix_latent[0], prefix_rope[0]
    )
    return out.reshape(64, steps, -1)


def solution(mesh):
    return jax.shard_map(
        body,
        mesh=mesh,
        in_specs=(
            P("grp", None, "tp", None),
            P("grp", None, None),
            P(),
            P("grp", None, None),
            P("grp", None, None),
            P("tp", None, None),
            P("tp", None, None),
            P("tp", "grp"),
        ),
        out_specs=P("tp", None, "grp"),
        check_vma=False,
    )
```

time: 658 us -> 150 us (0.23)
  waiting for transfers between devices: 547 us -> 0 us
  Pallas kernels: 0 us -> 142 us
  matrix products: 73.6 us -> 0 us
  other arithmetic: 18.7 us -> 0 us
  between operations: 14 us -> 0.66 us
    psum x1 -> x0, waiting for transfers between devices: 425 us -> none  [broadcast(): return lax.psum(jnp.where(mine, x, jnp.zeros_like(x)), axis)]
    pallas_call x0 -> x1, Pallas kernels: none -> 142 us  [layer(): pl.pallas_call(layer_kernel, out_shape=jax.ShapeDtypeStruct((4, 2, 32, 22...]
    all_gather x1 -> x0, waiting for transfers between devices: 105 us -> none  [body(): lax.all_gather(attended, 'grp', axis=0, tiled=True)]
    dot_general x9 -> x0, matrix products: 73.6 us -> none  [the longest x1 21.2 us: body(): jnp.dot(flat_rope, rotary, preferred_element_type=jnp.float32)]
    reduce_scatter x1 -> x0, waiting for transfers between devices: 16.8 us -> none  [body(): lax.psum_scatter(partial_terms.astype(jnp.bfloat16), 'tp', scatter_dimens...]
    reduce_sum x2 -> x0, other arithmetic: 13.8 us -> none  [the longest x1 13.6 us: body(): jnp.sum(prefix_exp, axis=1) + jnp.sum(new_exp, axis=3).reshape(row_count)]
  transfers between devices with their start and end apart: 3 -> 0, of which waited for: 3 -> 0; matrix products, arithmetic and copies ran while one was open for 1% -> 0% of each run, Pallas kernels for 0% -> 0%
where the time goes in v6:
time: 150 us; the launch traced here: 148 us
  Pallas kernels  142 us (95%)
  local copies, waits for them, and re-layouts  5.15 us (3%)
    pallas_call x1, Pallas kernels, layer(): pl.pallas_call(layer_kernel, out_shape=jax.ShapeDtypeStruct((4, 2, 32, 22...  142 us

profile of v6, /device:TPU:1, one launch (start us, length us, event | category | flops | bytes accessed | tf_op | source)
XLA Modules:
  0.0 147.9 jit_solution(15788901512385311112)
XLA Ops:
  0.7 1.4 reshape.14.new_ref
  2.1 2.1 %copy.9 = bf16[32,32,192]{2,0,1:T(8,128)(2,1)} copy(bf16[32,32,192]{2,1,0:T(8,128)(2,1)} %bitcast.13) | data formatting | bytes 786432 | tf_op jit(solution)/shard_map/reshape | solution.py:474
  4.2 142.1 %layer.1 = bf16[4,2,32,224]{3,2,1,0:T(8,128)(2,1)} custom-call(s32[1]{0:T(128)S(6)} %copy.10.owner_ref, bf16[1024,192]{1,0:T(8,128)(2,1)} %bitcast.10, bf16[32,576]{1,0:T(8,128)(2,1)} %reshape.14.new_ref, bf16[32,128,512]{2,1,0:T(8,128)(2,1)} %key_hbm.1, bf16[32,512,128]{2,1,0:T(8,128)(2,1)} %value_hbm.1, bf16[224,4096]{1,0:T(8,128)(2,1)} %bitcast.11, ...), custom_call_target="tpu_custom_call" | custom-call | tf_op jit(solution)/shard_map/layer/pallas_call | solution.py:459
  146.3 1.6 %reshape.15 = bf16[64,4,224]{2,1,0:T(4,128)(2,1)} reshape(bf16[4,2,32,224]{3,2,1,0:T(8,128)(2,1)} %layer.1) | data formatting | bytes 229376 | tf_op jit(solution)/shard_map/reshape | solution.py:478

commit v7 on v6

--- a/solution.py
+++ b/solution.py
@@ -26,17 +26,17 @@
 
 ORDERS = (("x", "y", "z"), ("y", "z", "x"), ("z", "x", "y"), ("z", "x", "y"))
 BASES = (0, 3072, 6144)
-SHARE = ((768, 192, 96), (768, 384, 96), (512, 128, 32), (2048, 512, 128))
+SHARE = ((768, 192, 96), (768, 384, 96), (512, 128, 32), (2048, 128))
 ROPE = 3
 
 
 def landing_shapes():
     shapes = []
     for region in range(4):
-        for step in range(3):
+        for step in range(2 if region == ROPE else 3):
             share = SHARE[region][step]
             one = (32, share) if region == ROPE else (share, 256 if region == 2 else 128)
-            slots = 2 if ORDERS[region][step] == "z" else 4
+            slots = 16 if (region, step) == (ROPE, 1) else 2 if ORDERS[region][step] == "z" else 4
             shapes.append(((slots,) + one, one))
     return shapes
 
@@ -46,9 +46,9 @@
 
 
 def layer_kernel(
-    owner_ref, q_ref, new_ref, key_hbm, value_hbm, weight_hbm, latent_hbm, rope_hbm, out_ref,
-    lat_ref, rot_ref, key_ref, value_ref, weight_ref, qlat_ref, acc_ref, max_ref, sum_ref,
-    att_ref, total_ref, part_ref, land_ref, local_sem, weight_send, weight_recv, sc_send, sc_recv, sc_own,
+    owner_ref, query_ref, fresh_ref, key_hbm, value_hbm, weight_hbm, latent_hbm, rope_hbm, out_ref,
+    q_ref, new_ref, wide_ref, lat_ref, rot_ref, key_ref, value_ref, weight_ref, qlat_ref, acc_ref, max_ref, sum_ref,
+    att_ref, total_ref, part_ref, land_ref, local_sem, weight_sem, sc_send, sc_recv, sc_own,
     ag_send, ag_recv, last_send, last_recv, sw_send, sw_recv, ex_send, ex_recv, rs_sem, *landings
 ):
     me = Coord()
@@ -163,13 +163,30 @@
     def gathered(region, level):
         wait_bytes(three(region, level), ag_recv.at[region * 3 + level - 1])
 
+    plane = [(i, j) for i in range(4) for j in range(4) if i or j]
+
+    def rope_scatter():
+        held, slots = landings[2 * 9 + 1], landings[2 * 10]
+        mine = me.x * 4 + me.y
+        for i, j in plane:
+            x, y = (me.x + i) % 4, (me.y + j) % 4
+            lanes = pl.ds(pl.multiple_of(128 * (x * 4 + y), 128), 128)
+            send(held.at[:, lanes], slots.at[mine], sc_send.at[10], sc_recv.at[10], me.at(x=x, y=y))
+        lanes = pl.ds(pl.multiple_of(128 * mine, 128), 128)
+        pltpu.make_async_copy(held.at[:, lanes], slots.at[mine], sc_own.at[10]).start()
+        drains.append((slots.at[0:15], sc_send.at[10]))
+
+    def rope_pick():
+        slots = landings[2 * 10]
+        wait_bytes(slots.at[0], sc_own.at[10])
+        wait_bytes(slots.at[0:15], sc_recv.at[10])
+        return slots[owner_digit["x"] * 4 + owner_digit["y"]]
+
     def rope_plane():
         ref = block(ROPE, 3, digits[ROPE])
         sems = ag_send.at[ROPE * 3 + 2], ag_recv.at[ROPE * 3 + 2]
-        for i in range(4):
-            for j in range(4):
-                if i or j:
-                    send(ref, ref, *sems, me.at(x=(me.x + i) % 4, y=(me.y + j) % 4))
+        for i, j in plane:
+            send(ref, ref, *sems, me.at(x=(me.x + i) % 4, y=(me.y + j) % 4))
         drains.append((rot_ref.at[0:32, 0:1920], sems[0]))
 
     def swap(d):
@@ -181,44 +198,57 @@
     def swapped(d):
         wait_bytes(lat_ref.at[0:2048, 0:256], sw_recv.at[d])
 
-    def send_weight(i):
-        where = pl.ds(i * CHUNK, CHUNK)
-        ref = weight_ref.at[zh, :, where]
-        send(weight_hbm.at[:, where], ref, weight_send.at[i], weight_recv.at[i], beside("z", 2))
-        drains.append((ref, weight_send.at[i]))
+    def send_weight(low, high):
+        where = pl.ds(16 * low, 16 * (high - low))
+        send(weight_hbm.at[where], weight_ref.at[zh, where], weight_sem.at[0], weight_sem.at[1], beside("z", 2))
 
     for region in range(4):
         scatter(region, 0)
     key_copy.start()
     value_copy.start()
     weight_copy.start()
+    wide_ref[...] = query_ref[...].astype(F32)
+
+    @pl.loop(0, 32, unroll=4)
+    def _(h):
+        q_ref[pl.ds(pl.multiple_of(h * 32, 32), 32), :] = wide_ref[:, h, :].astype(BF)
+
+    for sample in range(8):
+        wide_ref[0, 4 * sample : 4 * sample + 4, :] = fresh_ref[sample, :, 0:192].astype(F32)
+        wide_ref[1, 4 * sample : 4 * sample + 4, :] = fresh_ref[sample, :, 192:384].astype(F32)
+        wide_ref[2, 4 * sample : 4 * sample + 4, :] = fresh_ref[sample, :, 384:576].astype(F32)
+    for third in range(3):
+        new_ref[:, 192 * third : 192 * third + 192] = wide_ref[third].astype(BF)
     key_copy.wait()
     latent_queries(0, 16, q_ref, key_ref, qlat_ref)
-    for step in range(2):
-        for region in (ROPE, 0, 1, 2):
-            chosen = pick(region, step)
-            landings[2 * (region * 3 + step) + 1][...] = chosen
-            scatter(region, step + 1)
-        if step == 0:
-            send_weight(0)
-            latent_queries(16, 32, q_ref, key_ref, qlat_ref)
-    for region in (ROPE, 0, 1, 2):
+    landings[2 * 9 + 1][...] = pick(ROPE, 0)
+    rope_scatter()
+    for region in range(3):
+        landings[2 * (region * 3) + 1][...] = pick(region, 0)
+        scatter(region, 1)
+    send_weight(0, 1)
+    latent_queries(16, 32, q_ref, key_ref, qlat_ref)
+    home = block(ROPE, 3, digits[ROPE])
+    home[...] = rope_pick()
+    rope_plane()
+    for region in range(3):
+        landings[2 * (region * 3 + 1) + 1][...] = pick(region, 1)
+        scatter(region, 2)
+    send_weight(1, 2)
+    wait_bytes(rot_ref.at[0:32, 0:1920], ag_recv.at[ROPE * 3 + 2])
+    for region in range(3):
         home = block(region, 3, digits[region])
         home[...] = pick(region, 2)
-        if region == ROPE:
-            rope_plane()
-        else:
-            gather(region, 3)
-    send_weight(1)
+        gather(region, 3)
+    gather(ROPE, 1)
     new_keys(q_ref, new_ref, qlat_ref, acc_ref, max_ref, sum_ref)
-    wait_bytes(rot_ref.at[0:32, 0:1920], ag_recv.at[ROPE * 3 + 2])
-    gather(ROPE, 1)
     for region in range(3):
         gathered(region, 3)
         gather(region, 2)
     gathered(ROPE, 1)
     send(rot_ref.at[rope_rows], rot_ref.at[rope_rows], sw_send.at[4], sw_recv.at[4], me.at(c=1 - me.c))
     drains.append((rot_ref.at[0:32], sw_send.at[4]))
+    send_weight(2, 3)
     for region in range(3):
         gathered(region, 2)
         ref = block(region, 1, digits[region])
@@ -245,21 +275,25 @@
     wait_bytes(rot_ref.at[0:32], sw_recv.at[4])
     swapped(0)
 
-    @pl.loop(0, 2)
-    def _(i):
-        attend([(rows_of(2 * i), quarter(0)), (rows_of(2 * i + 1), quarter(0))])
-
+    def half(i, d):
+        attend([(rows_of(2 * i), quarter(d)), (rows_of(2 * i + 1), quarter(d))])
+
+    half(0, 0)
     arrived(1)
     swap(1)
-    send_weight(2)
-    send_weight(3)
+    half(1, 0)
     swapped(1)
-    for i in (0, 1):
-        attend([(rows_of(2 * i), quarter(1)), (rows_of(2 * i + 1), quarter(1))])
-        arrived((3, 2)[i])
-        swap((3, 2)[i])
+    half(0, 1)
+    arrived(3)
+    swap(3)
+    arrived(2)
+    swap(2)
+    send_weight(3, 5)
+    half(1, 1)
     swapped(3)
     swapped(2)
+    send_weight(5, 14)
+    drains.append((weight_ref.at[zh], weight_sem.at[0]))
 
     def exchange(chunk):
         cols = [pl.ds(chunk * CHUNK + lane * (CHUNK // 2), CHUNK // 2) for lane in (0, 1)]
@@ -276,12 +310,14 @@
         lines = [lambda y, s=slice(None): att_ref.at[s, y, :, cols[0]], lambda x, s=slice(None): att_ref.at[x, s, :, cols[1]]]
         for lane, axis in enumerate("yx"):
             ref = lines[lane](getattr(me, axis))
-            for d in (1, 3):
+            for d in (1, 3) if chunk < CHUNKS - 1 else (1, 3, 2):
                 send(ref, ref, *sems[1], beside(axis, d))
-        total = att_ref.at[0:2, :, :, whole]
+        total = att_ref.at[0 : 2 if chunk < CHUNKS - 1 else 3, :, :, whole]
         drains.append((total, sems[1][0]))
         yield
         wait_bytes(total, sems[1][1])
+        if chunk == CHUNKS - 1:
+            return
         for lane, axis in enumerate("yx"):
             for d, share in ((1, pl.ds(0, 2)), (3, pl.ds(2, 2))):
                 ref = lines[lane]((getattr(me, axis) + 4 - d) % 4, share)
@@ -312,18 +348,15 @@
     for chunk in range(CHUNKS - 1):
         for _ in active[chunk]:
             pass
-        wait_bytes(weight_ref.at[zh, :, pl.ds(chunk * CHUNK, CHUNK)], weight_recv.at[chunk])
+        if chunk == 0:
+            wait_bytes(weight_ref.at[zh], weight_sem.at[1])
 
         @pl.loop(0, 2)
         def _(half):
             term = partial_out(chunk, half)
             total_ref[half] = term if chunk == 0 else total_ref[half] + term
-
-        if chunk == 1:
-            next(active[3])
     for _ in active[-1]:
         pass
-    wait_bytes(weight_ref.at[zh, :, pl.ds(3 * CHUNK, CHUNK)], weight_recv.at[3])
     for far in (1, 0):
         half = 1 - zh if far else zh
         total_ref[half] = total_ref[half] + partial_out(CHUNKS - 1, half)
@@ -423,6 +456,9 @@
     sem = pltpu.SemaphoreType.DMA
     vm = pltpu.VMEM
     scratch = [
+        vm((1024, 192), BF),
+        vm((32, 576), BF),
+        vm((32, 32, 192), F32),
         vm((8192, 512), BF),
         vm((64, 8192), BF),
         vm((32, 128, 512), BF),
@@ -437,8 +473,7 @@
         vm((8, 128, 224), BF),
         vm((8, 128, 224), BF),
         sem((3,)),
-        sem((CHUNKS,)),
-        sem((CHUNKS,)),
+        sem((2,)),
         sem((12,)),
         sem((12,)),
         sem((12,)),
@@ -471,9 +506,9 @@
 
 def body(queries, new_kv, owner_index, prefix_latent, prefix_rope, key_up, value_up, out_weight):
     samples, steps, heads, width = queries.shape
-    rows = jnp.transpose(queries.reshape(samples * steps, heads, width), (1, 0, 2)).reshape(-1, width)
     out = layer(
-        owner_index, rows, new_kv.reshape(samples * steps, -1), key_up, value_up, out_weight.T, prefix_latent[0], prefix_rope[0]
+        owner_index, queries.reshape(samples * steps, heads, width), new_kv, key_up, value_up, out_weight.T,
+        prefix_latent[0], prefix_rope[0],
     )
     return out.reshape(64, steps, -1)
 

time: 150 us -> 116 us (0.77); the launches traced: 148 us -> 116 us
  Pallas kernels: 142 us -> 113 us
  local copies, waits for them, and re-layouts: 5.15 us -> 1.61 us
    pallas_call x1, Pallas kernels: 142 us -> 113 us  [layer(): pl.pallas_call(layer_kernel, out_shape=jax.ShapeDtypeStruct((4, 2, 32, 22...]
    reshape x2 -> x0, local copies, waits for them, and re-layouts: 3.54 us -> none  [the longest x1 2.12 us: body(): queries.reshape(samples * steps, heads, width)]
where the time goes in v7:
time: 116 us
  Pallas kernels  113 us (97%)
  local copies, waits for them, and re-layouts  1.61 us (1%)
    pallas_call x1, Pallas kernels, layer(): pl.pallas_call(layer_kernel, out_shape=jax.ShapeDtypeStruct((4, 2, 32, 22...  113 us

profile of v7, /device:TPU:1, one launch (start us, length us, event | category | flops | bytes accessed | tf_op | source)
XLA Modules:
  0.0 115.6 jit_solution(16216054832313227834)
XLA Ops:
  0.7 113.3 %layer.1 = bf16[4,2,32,224]{3,2,1,0:T(8,128)(2,1)} custom-call(s32[1]{0:T(128)S(6)} %copy.9.owner_ref, bf16[32,32,192]{2,1,0:T(8,128)(2,1)} %bitcast.9, bf16[8,4,576]{2,1,0:T(4,128)(2,1)} %fresh_ref.1, bf16[32,128,512]{2,1,0:T(8,128)(2,1)} %key_hbm.1, bf16[32,512,128]{2,1,0:T(8,128)(2,1)} %value_hbm.1, bf16[224,4096]{1,0:T(8,128)(2,1)} %bitcast.7, ...), custom_call_target="tpu_custom_call" | custom-call | tf_op jit(solution)/shard_map/layer/pallas_call | solution.py:494
  114.0 1.6 %reshape.7 = bf16[64,4,224]{2,1,0:T(4,128)(2,1)} reshape(bf16[4,2,32,224]{3,2,1,0:T(8,128)(2,1)} %layer.1) | data formatting | bytes 229376 | tf_op jit(solution)/shard_map/reshape | solution.py:513

commit v8 on v7

--- a/solution.py
+++ b/solution.py
@@ -201,6 +201,11 @@
     def send_weight(low, high):
         where = pl.ds(16 * low, 16 * (high - low))
         send(weight_hbm.at[where], weight_ref.at[zh, where], weight_sem.at[0], weight_sem.at[1], beside("z", 2))
+
+    def last(region, distances):
+        ref = block(region, 1, digits[region])
+        for d in distances:
+            send(ref, ref, last_send.at[d - 1], last_recv.at[d - 1], beside(ORDERS[region][0], d))
 
     for region in range(4):
         scatter(region, 0)
@@ -251,9 +256,7 @@
     send_weight(2, 3)
     for region in range(3):
         gathered(region, 2)
-        ref = block(region, 1, digits[region])
-        for d in (1, 3, 2):
-            send(ref, ref, last_send.at[d - 1], last_recv.at[d - 1], beside(ORDERS[region][0], d))
+        last(region, (1, 3))
     for d in (1, 2, 3):
         drains.append((lat_ref.at[0:2048, 0:256], last_send.at[d - 1]))
     swap(0)
@@ -279,13 +282,15 @@
         attend([(rows_of(2 * i), quarter(d)), (rows_of(2 * i + 1), quarter(d))])
 
     half(0, 0)
+    for region in range(3):
+        last(region, (2,))
+    half(1, 0)
     arrived(1)
     swap(1)
-    half(1, 0)
+    arrived(3)
+    swap(3)
     swapped(1)
     half(0, 1)
-    arrived(3)
-    swap(3)
     arrived(2)
     swap(2)
     send_weight(3, 5)

time: 116 us -> 115 us (level); the launches traced: 116 us -> 113 us
  Pallas kernels: 113 us -> 111 us
    pallas_call x1, Pallas kernels: 113 us -> 111 us  [layer(): pl.pallas_call(layer_kernel, out_shape=jax.ShapeDtypeStruct((4, 2, 32, 22...]
where the time goes in v8:
time: 115 us; the launch traced here: 113 us
  Pallas kernels  111 us (97%)
  local copies, waits for them, and re-layouts  1.61 us (1%)
    pallas_call x1, Pallas kernels, layer(): pl.pallas_call(layer_kernel, out_shape=jax.ShapeDtypeStruct((4, 2, 32, 22...  111 us

profile of v8, /device:TPU:1, one launch (start us, length us, event | category | flops | bytes accessed | tf_op | source)
XLA Modules:
  0.0 112.9 jit_solution(1943728816772409132)
XLA Ops:
  0.7 110.6 %layer.1 = bf16[4,2,32,224]{3,2,1,0:T(8,128)(2,1)} custom-call(s32[1]{0:T(128)S(6)} %copy.9.owner_ref, bf16[32,32,192]{2,1,0:T(8,128)(2,1)} %bitcast.9, bf16[8,4,576]{2,1,0:T(4,128)(2,1)} %fresh_ref.1, bf16[32,128,512]{2,1,0:T(8,128)(2,1)} %key_hbm.1, bf16[32,512,128]{2,1,0:T(8,128)(2,1)} %value_hbm.1, bf16[224,4096]{1,0:T(8,128)(2,1)} %bitcast.7, ...), custom_call_target="tpu_custom_call" | custom-call | tf_op jit(solution)/shard_map/layer/pallas_call | solution.py:499
  111.3 1.6 %reshape.7 = bf16[64,4,224]{2,1,0:T(4,128)(2,1)} reshape(bf16[4,2,32,224]{3,2,1,0:T(8,128)(2,1)} %layer.1) | data formatting | bytes 229376 | tf_op jit(solution)/shard_map/reshape | solution.py:518

commit v9 on v8

--- a/solution.py
+++ b/solution.py
@@ -294,7 +294,7 @@
     arrived(2)
     swap(2)
     send_weight(3, 5)
-    half(1, 1)
+    attend([(rows_of(2), quarter(1))])
     swapped(3)
     swapped(2)
     send_weight(5, 14)
@@ -339,7 +339,11 @@
     active = []
     for chunk in range(CHUNKS):
         rows = pl.ds(chunk * ROWS, ROWS)
-        attend([(rows, quarter(3)), (rows, quarter(2))])
+        if chunk == CHUNKS - 1:
+            attend([(rows, quarter(1)), (rows, quarter(3))])
+            attend([(rows, quarter(2))])
+        else:
+            attend([(rows, quarter(3)), (rows, quarter(2))])
         for other in active[-2:]:
             next(other)
         if chunk == 0:

time: 115 us -> 111 us (0.965); the launches traced: 113 us -> 111 us
  Pallas kernels: 111 us -> 108 us
    pallas_call x1, Pallas kernels: 111 us -> 108 us  [layer(): pl.pallas_call(layer_kernel, out_shape=jax.ShapeDtypeStruct((4, 2, 32, 22...]
where the time goes in v9:
time: 111 us
  Pallas kernels  108 us (97%)
  local copies, waits for them, and re-layouts  1.61 us (1%)
    pallas_call x1, Pallas kernels, layer(): pl.pallas_call(layer_kernel, out_shape=jax.ShapeDtypeStruct((4, 2, 32, 22...  108 us

profile of v9, /device:TPU:1, one launch (start us, length us, event | category | flops | bytes accessed | tf_op | source)
XLA Modules:
  0.0 110.7 jit_solution(12070408799835302650)
XLA Ops:
  0.7 108.4 %layer.1 = bf16[4,2,32,224]{3,2,1,0:T(8,128)(2,1)} custom-call(s32[1]{0:T(128)S(6)} %copy.9.owner_ref, bf16[32,32,192]{2,1,0:T(8,128)(2,1)} %bitcast.9, bf16[8,4,576]{2,1,0:T(4,128)(2,1)} %fresh_ref.1, bf16[32,128,512]{2,1,0:T(8,128)(2,1)} %key_hbm.1, bf16[32,512,128]{2,1,0:T(8,128)(2,1)} %value_hbm.1, bf16[224,4096]{1,0:T(8,128)(2,1)} %bitcast.7, ...), custom_call_target="tpu_custom_call" | custom-call | tf_op jit(solution)/shard_map/layer/pallas_call | solution.py:503
  109.1 1.6 %reshape.7 = bf16[64,4,224]{2,1,0:T(4,128)(2,1)} reshape(bf16[4,2,32,224]{3,2,1,0:T(8,128)(2,1)} %layer.1) | data formatting | bytes 229376 | tf_op jit(solution)/shard_map/reshape | solution.py:522
